TPU v7x, 32 devices: a whole 2x2x4 slice. The times are simulated.
32 devices in a mesh: slab: 4 (over y, x), tile: 8 (over z, core).
Axes of the slice: x: 2, y: 2, z: 4, core: 2. Of those that a mesh axis runs over, the one named last changes fastest.
Arguments:
- volume: float32 [16, 256, 1024], P('slab', 'tile'), may hold values from -6 to 6
Outputs:
- histogram: float32 [1, 16, 32, 64], P(None, 'tile', None, 'slab')
All inputs are finite; a program needn't handle non-finite values.
Results may differ from a plain program's by a relative error of at most 0.00005.
Values sent between devices are 32-bit elements; how exact they have to be, the bound alone decides.
A program may use at most 64 MiB of HBM per device.

v0:
```python
import jax
import jax.numpy as jnp
from jax import lax
from jax.sharding import PartitionSpec as P

RADIUS = 4
POOL = 16
DIRS = 32


def extended(cells, sides, width):
    for axis, dim in sides:
        count = lax.axis_size(axis)
        ends = count - 1
        head = lax.slice_in_dim(cells, 0, width, axis=dim)
        tail = lax.slice_in_dim(cells, cells.shape[dim] - width, cells.shape[dim], axis=dim)
        cells = jnp.concatenate(
            [
                lax.ppermute(tail, axis, [(i, (i + 1) % count) for i in range(ends)]),
                cells,
                lax.ppermute(head, axis, [((i + 1) % count, i) for i in range(ends)]),
            ],
            axis=dim,
        )
    return cells


def kernel_taps():
    offsets = jnp.arange(-RADIUS, RADIUS + 1).astype(jnp.float32)
    base = jnp.exp(-offsets * offsets / 8.0)
    smooth = base / jnp.sqrt(jnp.sum(base * base))
    slope = -offsets * base
    deriv = slope / jnp.sqrt(jnp.sum(slope * slope))
    return (smooth, deriv)


def direction_table():
    index = jnp.arange(DIRS).astype(jnp.float32)
    height = 1.0 - (index + 0.5) / DIRS
    radial = jnp.sqrt(1.0 - height * height)
    phase = 2.399963229728653 * index
    d_x = radial * jnp.cos(phase)
    d_y = radial * jnp.sin(phase)
    return jnp.stack(
        [
            height * height,
            2.0 * height * d_x,
            2.0 * height * d_y,
            d_x * d_x,
            2.0 * d_x * d_y,
            d_y * d_y,
        ],
        axis=1,
    )


def filtered(padded, weights, axis, count):
    total = weights[0] * lax.slice_in_dim(padded, 0, count, axis=axis)
    for shift_index in range(1, 2 * RADIUS + 1):
        total = total + weights[shift_index] * lax.slice_in_dim(
            padded, shift_index, shift_index + count, axis=axis
        )
    return total


def pooled_full(field):
    planes, rows, cells = field.shape
    return field.reshape(planes // POOL, POOL, rows // POOL, POOL, cells // POOL, POOL).sum(
        axis=(1, 3, 5)
    )


def body(volume):
    smooth, deriv = kernel_taps()
    planes, rows, cells = volume.shape
    coeffs = direction_table()
    regrouped = lax.all_to_all(volume, "slab", split_axis=2, concat_axis=0, tiled=True)
    depth = regrouped.shape[0]
    owned = regrouped.shape[2]
    padded = extended(regrouped, (("slab", 2), ("tile", 1)), RADIUS)
    zpad = jnp.pad(padded, ((RADIUS, RADIUS), (0, 0), (0, 0)))
    z_smooth = filtered(zpad, smooth, 0, depth)
    z_deriv = filtered(zpad, deriv, 0, depth)
    both_smooth = filtered(z_smooth, smooth, 1, rows)
    smooth_deriv = filtered(z_smooth, deriv, 1, rows)
    deriv_smooth = filtered(z_deriv, smooth, 1, rows)
    grad_y = filtered(both_smooth, deriv, 2, owned)
    grad_x = filtered(smooth_deriv, smooth, 2, owned)
    grad_z = filtered(deriv_smooth, smooth, 2, owned)
    tensor = jnp.stack(
        [
            pooled_full(grad_z * grad_z),
            pooled_full(grad_z * grad_x),
            pooled_full(grad_z * grad_y),
            pooled_full(grad_x * grad_x),
            pooled_full(grad_x * grad_y),
            pooled_full(grad_y * grad_y),
        ]
    )
    hist = jnp.einsum("kc,cabv->abkv", coeffs, tensor, precision=lax.Precision.HIGHEST)
    return hist / float(POOL**3)


def solution(mesh):
    return jax.shard_map(
        body,
        mesh=mesh,
        in_specs=(P("slab", "tile", None),),
        out_specs=P(None, "tile", None, "slab"),
        check_vma=False,
    )
```

profile of v0, /device:TPU:1, one launch (start us, length us, event | category | flops | bytes accessed | tf_op | source)
XLA Modules:
  0.0 95.2 jit_solution(15103473297895418354)
XLA Ops:
  0.0 1.8 %copy.30 = f32[4,32,1024]{1,0,2:T(4,128)S(1)} copy(f32[4,32,1024]{2,1,0:T(8,128)} %param.1) | data formatting | bytes 1048576 | tf_op args[0]
  1.8 2.1 %reshape.98 = f32[4,1,32768]{2,1,0:T(1,128)} reshape(f32[1024,4,32]{2,1,0:T(4,128)S(1)} %bitcast.54) | data formatting | bytes 1048576
  3.8 4.3 %all-to-all-start = ((f32[4,1,32768]{2,1,0:T(1,128)}), f32[4,1,32768]{2,1,0:T(1,128)S(1)}, u32[]{:S(2)}, u32[]{:S(2)}) async-start(f32[4,1,32768]{2,1,0:T(1,128)} %reshape.98), calls=%async_computation | async-start | bytes 1048576 | tf_op jit(solution)/shard_map/all_to_all | solution.py:77
  8.1 0.7 multiply_reduce_fusion.6
  8.8 0.6 multiply_reduce_fusion.7
  11.0 0.7 fusion.41
  11.7 3.6 %all-to-all-done = f32[4,1,32768]{2,1,0:T(1,128)S(1)} async-done(((f32[4,1,32768]{2,1,0:T(1,128)}), f32[4,1,32768]{2,1,0:T(1,128)S(1)}, u32[]{:S(2)}, u32[]{:S(2)}) %all-to-all-start) | async-done | bytes 524320 | tf_op jit(solution)/shard_map/all_to_all | solution.py:77
  15.2 0.5 broadcast.224
  15.7 2.1 %reduce.18 = f32[4,32768]{1,0:T(4,128)S(1)} reduce(f32[4,1,32768]{2,1,0:T(1,128)S(1)} %all-to-all-done, f32[]{:T(128)} %broadcast.224), dimensions={1}, to_apply=%all_to_all.13.reduce_sub_computation | reduce | bytes 1048580 | tf_op jit(solution)/shard_map/all_to_all | solution.py:77
  17.9 1.1 %reshape.99 = f32[1024,4,32]{2,1,0:T(4,128)S(1)} reshape(f32[4,32768]{1,0:T(4,128)S(1)} %reduce.18) | data formatting | bytes 1048576
  19.0 0.8 copy.32
  19.8 0.1 fusion.40
  20.0 2.7 %collective-permute-start = (f32[16,32,4]{2,1,0:T(8,128)S(1)}, f32[16,32,4]{2,1,0:T(8,128)S(1)}, u32[]{:S(2)}, u32[]{:S(2)}) collective-permute-start(f32[16,32,4]{2,1,0:T(8,128)S(1)} %get-tuple-element.13), channel_id=1, source_target_pairs={{0,8},{8,16},{16,24},{1,9},{9,17},{17,25},{2,10},{10,18},{18,26},{... | collective-permute-start | bytes 24584 | tf_op jit(solution)/shard_map/ppermute | solution.py:19
  22.7 1.3 %collective-permute-start.1 = (f32[16,32,4]{2,1,0:T(8,128)S(1)}, f32[16,32,4]{2,1,0:T(8,128)S(1)}, u32[]{:S(2)}, u32[]{:S(2)}) collective-permute-start(f32[16,32,4]{2,1,0:T(8,128)S(1)} %get-tuple-element.14), channel_id=1, source_target_pairs={{8,0},{16,8},{24,16},{9,1},{17,9},{25,17},{10,2},{18,10},{26,18},{... | collective-permute-start | bytes 24584 | tf_op jit(solution)/shard_map/ppermute | solution.py:21
  24.0 1.9 %collective-permute-done = f32[16,32,4]{2,1,0:T(8,128)S(1)} collective-permute-done((f32[16,32,4]{2,1,0:T(8,128)S(1)}, f32[16,32,4]{2,1,0:T(8,128)S(1)}, u32[]{:S(2)}, u32[]{:S(2)}) %collective-permute-start) | collective-permute-done | bytes 8224 | tf_op jit(solution)/shard_map/ppermute | solution.py:19
  26.0 8.4 %collective-permute-done.1 = f32[16,32,4]{2,1,0:T(8,128)S(1)} collective-permute-done((f32[16,32,4]{2,1,0:T(8,128)S(1)}, f32[16,32,4]{2,1,0:T(8,128)S(1)}, u32[]{:S(2)}, u32[]{:S(2)}) %collective-permute-start.1) | collective-permute-done | bytes 8224 | tf_op jit(solution)/shard_map/ppermute | solution.py:21
  34.3 0.2 pad_maximum_fusion.3
  34.6 5.8 %collective-permute-start.2 = (f32[16,4,264]{2,1,0:T(4,128)S(1)}, f32[16,4,264]{2,1,0:T(4,128)S(1)}, u32[]{:S(2)}, u32[]{:S(2)}) collective-permute-start(f32[16,4,264]{2,1,0:T(4,128)S(1)} %get-tuple-element.11), channel_id=1, source_target_pairs={{0,1},{1,2},{2,3},{3,4},{4,5},{5,6},{6,7},{8,9},{9,10},{10,11},{11... | collective-permute-start | bytes 202760 | tf_op jit(solution)/shard_map/ppermute | solution.py:19
  40.4 1.9 %collective-permute-start.3 = (f32[16,4,264]{2,1,0:T(4,128)S(1)}, f32[16,4,264]{2,1,0:T(4,128)S(1)}, u32[]{:S(2)}, u32[]{:S(2)}) collective-permute-start(f32[16,4,264]{2,1,0:T(4,128)S(1)} %get-tuple-element.12), channel_id=1, source_target_pairs={{1,0},{2,1},{3,2},{4,3},{5,4},{6,5},{7,6},{9,8},{10,9},{11,10},{12... | collective-permute-start | bytes 202760 | tf_op jit(solution)/shard_map/ppermute | solution.py:21
  42.3 0.7 fusion.42
  43.0 0.0 collective-permute-done.2
  43.0 3.3 %collective-permute-done.3 = f32[16,4,264]{2,1,0:T(4,128)S(1)} collective-permute-done((f32[16,4,264]{2,1,0:T(4,128)S(1)}, f32[16,4,264]{2,1,0:T(4,128)S(1)}, u32[]{:S(2)}, u32[]{:S(2)}) %collective-permute-start.3) | collective-permute-done | bytes 67616 | tf_op jit(solution)/shard_map/ppermute | solution.py:21
  46.3 0.4 pad_maximum_fusion
  46.8 6.1 %multiply_add_fusion.1 = f32[16,40,264]{2,1,0:T(8,128)S(1)} fusion(f32[16,40,264]{2,1,0:T(8,128)S(1)} %pad_maximum_fusion, f32[]{:T(128)} %bitcast.14, f32[]{:T(128)} %bitcast.13, f32[]{:T(128)} %bitcast.12, f32[]{:T(128)} %bitcast.11, f32[]{:T(128)} %bitcast.10, f32[]{:T(128)} %bitcast.9, f32[]{:T(128)} %bitcast.8, f32[]{:T(128)} %bitcast.7, f32[]{:T(128)} %bitcast.1), kind=kLoop, calls=%fused_computation.12 | loop fusion | flops 2872320 | bytes 1351716 | tf_op jit(solution)/shard_map/add | solution.py:60
  52.9 6.1 %multiply_add_fusion = f32[16,40,264]{2,1,0:T(8,128)S(1)} fusion(f32[16,40,264]{2,1,0:T(8,128)S(1)} %pad_maximum_fusion, f32[]{:T(128)} %bitcast.22, f32[]{:T(128)} %bitcast.21, f32[]{:T(128)} %bitcast.20, f32[]{:T(128)} %bitcast.19, f32[]{:T(128)} %bitcast.18, f32[]{:T(128)} %bitcast.17, f32[]{:T(128)} %bitcast.16, f32[]{:T(128)} %bitcast.15, f32[]{:T(128)} %bitcast), kind=kLoop, calls=%fused_computation.11 | loop fusion | flops 2872320 | bytes 1351716 | tf_op jit(solution)/shard_map/add | solution.py:60
  59.0 6.4 %multiply_add_fusion.3 = f32[16,32,264]{2,1,0:T(8,128)S(1)} fusion(f32[16,40,264]{2,1,0:T(8,128)S(1)} %multiply_add_fusion, f32[]{:T(128)} %bitcast.14, f32[]{:T(128)} %bitcast.13, f32[]{:T(128)} %bitcast.12, f32[]{:T(128)} %bitcast.11, f32[]{:T(128)} %bitcast.10, f32[]{:T(128)} %bitcast.9, f32[]{:T(128)} %bitcast.8, f32[]{:T(128)} %bitcast.7, f32[]{:T(128)} %bitcast.1), kind=kLoop, calls=%fused_computation.31 | loop fusion | flops 2297856 | bytes 5406756 | tf_op jit(solution)/shard_map/add | solution.py:60
  65.4 6.4 %multiply_add_fusion.2 = f32[16,32,264]{2,1,0:T(8,128)S(1)} fusion(f32[16,40,264]{2,1,0:T(8,128)S(1)} %multiply_add_fusion, f32[]{:T(128)} %bitcast.22, f32[]{:T(128)} %bitcast.21, f32[]{:T(128)} %bitcast.20, f32[]{:T(128)} %bitcast.19, f32[]{:T(128)} %bitcast.18, f32[]{:T(128)} %bitcast.17, f32[]{:T(128)} %bitcast.16, f32[]{:T(128)} %bitcast.15, f32[]{:T(128)} %bitcast), kind=kLoop, calls=%fused_computation.30 | loop fusion | flops 2297856 | bytes 5406756 | tf_op jit(solution)/shard_map/add | solution.py:60
  71.8 6.4 %fusion.1 = f32[16,32,264]{2,1,0:T(8,128)S(1)} fusion(f32[16,40,264]{2,1,0:T(8,128)S(1)} %multiply_add_fusion.1, f32[]{:T(128)} %bitcast.22, f32[]{:T(128)} %bitcast.21, f32[]{:T(128)} %bitcast.20, f32[]{:T(128)} %bitcast.19, f32[]{:T(128)} %bitcast.18, f32[]{:T(128)} %bitcast.17, f32[]{:T(128)} %bitcast.16, f32[]{:T(128)} %bitcast.15, f32[]{:T(128)} %bitcast), kind=kLoop, calls=%fused_computation.14 | loop fusion | flops 2297856 | bytes 5406756 | tf_op jit(solution)/shard_map/add | solution.py:60
  78.2 14.6 %multiply_reduce_fusion = (f32[32,256]{1,0:T(8,128)S(1)}, f32[32,256]{1,0:T(8,128)S(1)}, f32[32,256]{1,0:T(8,128)S(1)}, f32[32,256]{1,0:T(8,128)S(1)}, f32[32,256]{1,0:T(8,128)S(1)}, /*index=5*/f32[32,256]{1,0:T(8,128)S(1)}) fusion(f32[16,32,264]{2,1,0:T(8,128)S(1)} %multiply_add_fusion.2, f32[]{:T(128)} %bitcast.14, f32[]{:T(128)} %bitcast.13, f32[]{:T(128)} %bitcast.12, ...), kind=kLoop, calls=%fused_computation.83 | loop fusion | flops 8208384 | bytes 14352456 | tf_op jit(solution)/shard_map/reduce_sum | solution.py:68
  92.9 0.1 reduce_sum.91
  93.0 0.1 reduce_sum.97
  93.1 0.1 reduce_sum.95
  93.2 0.1 reduce_sum.98
  93.4 0.1 reduce_sum.103
  93.5 0.1 reduce_sum.124
  93.6 0.1 reduce_sum.126
  93.7 0.1 reduce_sum.127
  93.8 0.1 reduce_sum.129
  94.0 0.1 reduce_sum.130
  94.1 0.1 reduce_sum.132
  94.2 0.1 reduce_sum.133
  94.4 0.8 fusion
  (7 shorter events, 0.2 us)
Async XLA Ops:
  3.8 11.4 %all-to-all-start = ((f32[4,1,32768]{2,1,0:T(1,128)}), f32[4,1,32768]{2,1,0:T(1,128)S(1)}, u32[]{:S(2)}, u32[]{:S(2)}) async-start(f32[4,1,32768]{2,1,0:T(1,128)} %reshape.98), calls=%async_computation | async-start | bytes 1048576 | tf_op jit(solution)/shard_map/all_to_all | solution.py:77
  20.0 6.0 %collective-permute-start = (f32[16,32,4]{2,1,0:T(8,128)S(1)}, f32[16,32,4]{2,1,0:T(8,128)S(1)}, u32[]{:S(2)}, u32[]{:S(2)}) collective-permute-start(f32[16,32,4]{2,1,0:T(8,128)S(1)} %get-tuple-element.13), channel_id=1, source_target_pairs={{0,8},{8,16},{16,24},{1,9},{9,17},{17,25},{2,10},{10,18},{18,26},{... | collective-permute-start | bytes 24584 | tf_op jit(solution)/shard_map/ppermute | solution.py:19
  22.7 11.7 %collective-permute-start.1 = (f32[16,32,4]{2,1,0:T(8,128)S(1)}, f32[16,32,4]{2,1,0:T(8,128)S(1)}, u32[]{:S(2)}, u32[]{:S(2)}) collective-permute-start(f32[16,32,4]{2,1,0:T(8,128)S(1)} %get-tuple-element.14), channel_id=1, source_target_pairs={{8,0},{16,8},{24,16},{9,1},{17,9},{25,17},{10,2},{18,10},{26,18},{... | collective-permute-start | bytes 24584 | tf_op jit(solution)/shard_map/ppermute | solution.py:21
  34.6 8.5 %collective-permute-start.2 = (f32[16,4,264]{2,1,0:T(4,128)S(1)}, f32[16,4,264]{2,1,0:T(4,128)S(1)}, u32[]{:S(2)}, u32[]{:S(2)}) collective-permute-start(f32[16,4,264]{2,1,0:T(4,128)S(1)} %get-tuple-element.11), channel_id=1, source_target_pairs={{0,1},{1,2},{2,3},{3,4},{4,5},{5,6},{6,7},{8,9},{9,10},{10,11},{11... | collective-permute-start | bytes 202760 | tf_op jit(solution)/shard_map/ppermute | solution.py:19
  40.4 5.9 %collective-permute-start.3 = (f32[16,4,264]{2,1,0:T(4,128)S(1)}, f32[16,4,264]{2,1,0:T(4,128)S(1)}, u32[]{:S(2)}, u32[]{:S(2)}) collective-permute-start(f32[16,4,264]{2,1,0:T(4,128)S(1)} %get-tuple-element.12), channel_id=1, source_target_pairs={{1,0},{2,1},{3,2},{4,3},{5,4},{6,5},{7,6},{9,8},{10,9},{11,10},{12... | collective-permute-start | bytes 202760 | tf_op jit(solution)/shard_map/ppermute | solution.py:21
where the time goes:
time: 96 us; the launch traced here: 95.2 us
  other arithmetic  50.9 us (53%)
  waiting for transfers between devices  17.2 us (18%)
  starting transfers between devices  16 us (17%)
  local copies, waits for them, and re-layouts  8.54 us (9%)
  between operations  1.62 us (2%)
    add x5, other arithmetic, filtered(): total + weights[shift_index] * lax.slice_in_dim(padded, shift_index, shif...  31.4 us
    reduce_sum x7, other arithmetic, pooled_full(): field.reshape(planes // POOL, POOL, rows // POOL, POOL, cells // POOL, POOL)  15.3 us
    ppermute x2, waiting for transfers between devices, extended(): lax.ppermute(head, axis, [((i + 1) % count, i) for i in range(ends)])  11.7 us
    ppermute x2, starting transfers between devices, extended(): lax.ppermute(tail, axis, [(i, (i + 1) % count) for i in range(ends)])  8.57 us
    unnamed x3, local copies, waits for them, and re-layouts  4.95 us
    all_to_all x1, starting transfers between devices, body(): lax.all_to_all(volume, 'slab', split_axis=2, concat_axis=0, tiled=True)  4.27 us
    all_to_all x1, waiting for transfers between devices, body(): lax.all_to_all(volume, 'slab', split_axis=2, concat_axis=0, tiled=True)  3.57 us
    ppermute x2, starting transfers between devices, extended(): lax.ppermute(head, axis, [((i + 1) % count, i) for i in range(ends)])  3.21 us
  transfers between devices with their start and end apart: 5, of which 4 were waited for; matrix products, arithmetic and copies ran while one was open for 3% of the time, Pallas kernels for 0%

commit v1 on v0

--- a/solution.py
+++ b/solution.py
@@ -1,11 +1,20 @@
+import functools
+
 import jax
 import jax.numpy as jnp
+import ml_dtypes
+import numpy as np
 from jax import lax
+from jax.experimental import pallas as pl
+from jax.experimental.pallas import tpu as pltpu
 from jax.sharding import PartitionSpec as P
 
 RADIUS = 4
 POOL = 16
 DIRS = 32
+MESH = pl.DeviceIdType.MESH
+LANES = 128
+EDGE = 2 * RADIUS
 
 
 def extended(cells, sides, width):
@@ -101,9 +110,376 @@
     return hist / float(POOL**3)
 
 
+def host_taps():
+    offsets = np.arange(-RADIUS, RADIUS + 1).astype(np.float64)
+    base = np.exp(-offsets * offsets / 8.0)
+    slope = -offsets * base
+    return base / np.sqrt(np.sum(base * base)), slope / np.sqrt(np.sum(slope * slope))
+
+
+def host_directions():
+    index = np.arange(DIRS).astype(np.float32)
+    height = np.float32(1.0) - (index + np.float32(0.5)) / np.float32(DIRS)
+    radial = np.sqrt(np.float32(1.0) - height * height)
+    phase = np.float32(2.399963229728653) * index
+    d_x = radial * np.cos(phase)
+    d_y = radial * np.sin(phase)
+    two = np.float32(2.0)
+    return np.stack(
+        [height * height, two * height * d_x, two * height * d_y, d_x * d_x, two * d_x * d_y, d_y * d_y],
+        axis=1,
+    ).astype(np.float32)
+
+
+def tap_at(weights, distance):
+    index = distance + RADIUS
+    inside = (index >= 0) & (index <= 2 * RADIUS)
+    return np.where(inside, weights[np.clip(index, 0, 2 * RADIUS)], 0.0)
+
+
+def halves(matrix):
+    high = matrix.astype(np.float32).astype(ml_dtypes.bfloat16)
+    low = (matrix - high.astype(np.float64)).astype(np.float32).astype(ml_dtypes.bfloat16)
+    return np.stack([high, low])
+
+
+def row_places(planes, rows):
+    z, x = np.meshgrid(np.arange(planes), np.arange(rows), indexing="ij")
+    parts = [(RADIUS, rows - RADIUS), (0, RADIUS), (rows - RADIUS, rows)]
+    places = [(z[:, a:b].ravel(), x[:, a:b].ravel()) for a, b in parts]
+    near, step = np.meshgrid(np.arange(planes), np.arange(RADIUS), indexing="ij")
+    places.append((near.ravel(), step.ravel() - RADIUS))
+    places.append((near.ravel(), step.ravel() + rows))
+    return np.concatenate([p[0] for p in places]), np.concatenate([p[1] for p in places])
+
+
+def y_weights(owned):
+    smooth, deriv = host_taps()
+    edge = np.concatenate([np.arange(-RADIUS, 0), owned + np.arange(RADIUS)])
+    out = np.arange(owned)
+    table = np.zeros((owned + LANES, 2 * owned))
+    for column, weights in enumerate((smooth, deriv)):
+        span = slice(column * owned, (column + 1) * owned)
+        table[:owned, span] = tap_at(weights, out[:, None] - out[None, :])
+        for copy in range(3):
+            start = owned + copy * EDGE
+            table[start : start + EDGE, span] = tap_at(weights, edge[:, None] - out[None, :])
+    return halves(table)
+
+
+def zx_weights(planes, rows):
+    smooth, deriv = host_taps()
+    z_in, x_in = row_places(planes, rows)
+    z_out, x_out = (g.ravel() for g in np.meshgrid(np.arange(planes), np.arange(rows), indexing="ij"))
+    fields = []
+    for z_taps, x_taps in ((deriv, smooth), (smooth, deriv), (smooth, smooth)):
+        blocks = []
+        for group in (-1, 0, 1):
+            along_z = tap_at(z_taps, group * planes + z_in[None, :] - z_out[:, None])
+            blocks.append(along_z * tap_at(x_taps, x_in[None, :] - x_out[:, None]))
+        fields.append(np.concatenate(blocks, axis=1))
+    return halves(np.concatenate(fields, axis=0))
+
+
+def histogram_weights(rows):
+    voxels = rows // POOL
+    inside = (np.arange(rows)[None, :] // POOL == np.arange(voxels)[:, None]).astype(np.float32)
+    table = host_directions()[None, :, :, None] * inside[:, None, None, :]
+    return (table.reshape(voxels * DIRS, -1) / np.float32(POOL**3)).astype(np.float32)
+
+
+def split(values):
+    high = values.astype(jnp.bfloat16)
+    low = (values - high.astype(jnp.float32)).astype(jnp.bfloat16)
+    return high, low
+
+
+def dot(a, b):
+    return jnp.dot(a, b, preferred_element_type=jnp.float32)
+
+
+def exact_dot(a, b):
+    return jnp.dot(a, b, preferred_element_type=jnp.float32, precision=lax.Precision.HIGHEST)
+
+
+def kernel(
+    slabs, tiles, x_hbm, wy_hbm, wzx_hbm, whist_ref, out_ref,
+    x_ref, wy_ref, wzx_ref, stage, recv, halo_l, halo_r, y_high, y_low,
+    load_sem, send_sem, recv_sem, fl_send, fl_recv, fr_send, fr_recv,
+):
+    planes, rows, cells = x_ref.shape
+    owned = cells // slabs
+    band = planes * RADIUS
+    body_rows = planes * rows
+    mid = body_rows - 2 * band
+    e_at = mid + band
+    total = body_rows + 2 * band
+    s = lax.axis_index("slab")
+    t = lax.axis_index("tile")
+    has_left = t > 0
+    has_right = t < tiles - 1
+
+    loads = [
+        pltpu.make_async_copy(src, dst, load_sem.at[i])
+        for i, (src, dst) in enumerate(((x_hbm, x_ref), (wy_hbm, wy_ref), (wzx_hbm, wzx_ref)))
+    ]
+    for load in loads:
+        load.start()
+
+    barrier = pltpu.get_barrier_semaphore()
+    for k in range(1, slabs):
+        pl.semaphore_signal(barrier, inc=1, device_id=(lax.rem(s + k, slabs), t), device_id_type=MESH)
+
+    @pl.when(has_left)
+    def _():
+        pl.semaphore_signal(barrier, inc=1, device_id=(s, t - 1), device_id_type=MESH)
+
+    @pl.when(has_right)
+    def _():
+        pl.semaphore_signal(barrier, inc=1, device_id=(s, t + 1), device_id_type=MESH)
+
+    loads[0].wait()
+    for d in range(slabs):
+        span = slice(d * owned, (d + 1) * owned)
+        for z in range(planes):
+            inner = rows - 2 * RADIUS
+            stage[d, z * inner : (z + 1) * inner, :] = x_ref[z, RADIUS : rows - RADIUS, span]
+        top = [x_ref[z, 0:RADIUS, span] for z in range(planes)]
+        bottom = [x_ref[z, rows - RADIUS : rows, span] for z in range(planes)]
+        stage[d, mid : mid + band, :] = jnp.concatenate(top, axis=0)
+        stage[d, e_at + EDGE : e_at + EDGE + band, :] = jnp.concatenate(bottom, axis=0)
+
+    lane = lax.broadcasted_iota(jnp.int32, (body_rows, LANES), 1)
+    nothing = jnp.zeros((body_rows, LANES), jnp.float32)
+
+    def side(d, lanes):
+        if d < 0 or d >= slabs:
+            return nothing
+        return jnp.concatenate(
+            [stage[d, 0:e_at, lanes], stage[d, e_at + EDGE : e_at + EDGE + band, lanes]], axis=0
+        )
+
+    edges = nothing
+    for d in range(slabs):
+        before = side(d - 1, slice(owned - LANES, owned))
+        after = side(d + 1, slice(0, LANES))
+        both = jnp.where(lane >= LANES // 2, before, after)
+        turned = pltpu.roll(both, d * EDGE + RADIUS, 1)
+        edges = jnp.where(lane // EDGE == d, turned, edges)
+    edges = edges.T
+    for d in range(slabs):
+        stage[d, e_at : e_at + EDGE, 0:LANES] = edges[d * EDGE : (d + 1) * EDGE]
+        stage[d, e_at : e_at + EDGE, LANES:] = jnp.zeros((EDGE, owned - LANES), jnp.float32)
+
+    beside = jnp.where(has_left, 1, 0) + jnp.where(has_right, 1, 0)
+    pl.semaphore_wait(barrier, slabs - 1 + beside)
+
+    def to_peer(k):
+        peer = lax.rem(s + k, slabs)
+        return pltpu.make_async_remote_copy(
+            src_ref=stage.at[peer], dst_ref=recv.at[s],
+            send_sem=send_sem.at[k], recv_sem=recv_sem.at[s],
+            device_id=(peer, t), device_id_type=MESH,
+        )
+
+    def from_peer(p):
+        return pltpu.make_async_remote_copy(
+            src_ref=stage.at[p], dst_ref=recv.at[p],
+            send_sem=send_sem.at[0], recv_sem=recv_sem.at[p],
+            device_id=(p, t), device_id_type=MESH,
+        )
+
+    def to_left(p):
+        return pltpu.make_async_remote_copy(
+            src_ref=recv.at[p, pl.ds(mid, band + EDGE)], dst_ref=halo_r.at[p],
+            send_sem=fl_send.at[p], recv_sem=fl_recv.at[p],
+            device_id=(s, t - 1), device_id_type=MESH,
+        )
+
+    def to_right(p):
+        return pltpu.make_async_remote_copy(
+            src_ref=recv.at[p, pl.ds(e_at, band + EDGE)], dst_ref=halo_l.at[p],
+            send_sem=fr_send.at[p], recv_sem=fr_recv.at[p],
+            device_id=(s, t + 1), device_id_type=MESH,
+        )
+
+    sends = [to_peer(k) for k in range(1, slabs)]
+    for send in sends:
+        send.start()
+
+    def forward(p):
+        @pl.when(has_left)
+        def _():
+            to_left(p).start()
+
+        @pl.when(has_right)
+        def _():
+            to_right(p).start()
+
+    recv[s] = stage[s]
+    forward(s)
+
+    @pl.when(jnp.logical_not(has_left))
+    def _():
+        halo_l[...] = jnp.zeros_like(halo_l)
+
+    @pl.when(jnp.logical_not(has_right))
+    def _():
+        halo_r[...] = jnp.zeros_like(halo_r)
+
+    for ref in (y_high, y_low):
+        ref[0:total, :] = jnp.zeros((total, 2 * owned), jnp.bfloat16)
+        ref[(slabs + 1) * total : (slabs + 2) * total, :] = jnp.zeros((total, 2 * owned), jnp.bfloat16)
+
+    lane = lax.broadcasted_iota(jnp.int32, (total, LANES), 1)
+    row = lax.broadcasted_iota(jnp.int32, (total, LANES), 0)
+    owner = jnp.where(row < body_rows, 0, jnp.where(row < body_rows + band, 1, 2))
+    own_edge = lane // EDGE == owner
+
+    def along_y(p):
+        @pl.when(has_left)
+        def _():
+            to_right(p).wait_recv()
+
+        @pl.when(has_right)
+        def _():
+            to_left(p).wait_recv()
+
+        block = jnp.concatenate(
+            [
+                recv[p, 0:e_at, :],
+                recv[p, e_at + EDGE : e_at + EDGE + band, :],
+                halo_l[p, EDGE : EDGE + band, :],
+                halo_r[p, 0:band, :],
+            ],
+            axis=0,
+        )
+        ends = jnp.concatenate(
+            [
+                recv[p, e_at : e_at + EDGE, 0:LANES],
+                halo_l[p, 0:EDGE, 0:LANES],
+                halo_r[p, band : band + EDGE, 0:LANES],
+                jnp.zeros((LANES - 3 * EDGE, LANES), jnp.float32),
+            ],
+            axis=0,
+        ).T
+        ends = jnp.concatenate([ends, ends[e_at : e_at + band], ends[mid : mid + band]], axis=0)
+        ends = jnp.where(own_edge, ends, 0.0)
+        high, low = split(jnp.concatenate([block, ends], axis=1))
+        result = dot(high, wy_ref[0]) + dot(low, wy_ref[0]) + dot(high, wy_ref[1])
+        high, low = split(result)
+        at = pl.ds(pl.multiple_of((p + 1) * total, 16), total)
+        y_high[at, :] = high
+        y_low[at, :] = low
+
+    loads[1].wait()
+    loads[2].wait()
+    for k in range(1, slabs):
+        p = lax.rem(s + slabs - k, slabs)
+        from_peer(p).wait_recv()
+        forward(p)
+        along_y(lax.rem(p + 1, slabs))
+    along_y(lax.rem(s + 1, slabs))
+
+    sums = [jnp.zeros((rows, owned), jnp.float32) for _ in range(6)]
+
+    def group(g, sums):
+        at = pl.ds(pl.multiple_of(g * total, 16), 3 * total)
+        smooth_y = slice(0, owned)
+        deriv_y = slice(owned, 2 * owned)
+        two = slice(0, 2 * body_rows)
+        one = slice(2 * body_rows, 3 * body_rows)
+
+        def gradient(out, field):
+            high = y_high[at, field]
+            low = y_low[at, field]
+            return dot(wzx_ref[0, out, :], high) + dot(wzx_ref[0, out, :], low) + dot(wzx_ref[1, out, :], high)
+
+        pair = gradient(two, smooth_y)
+        grad_z = pair[:body_rows]
+        grad_x = pair[body_rows:]
+        grad_y = gradient(one, deriv_y)
+        products = (
+            grad_z * grad_z, grad_z * grad_x, grad_z * grad_y,
+            grad_x * grad_x, grad_x * grad_y, grad_y * grad_y,
+        )
+        return tuple(
+            held + product.reshape(planes, rows, owned).sum(axis=0)
+            for held, product in zip(sums, products)
+        )
+
+    sums = lax.fori_loop(0, slabs, group, tuple(sums))
+    mixed = exact_dot(whist_ref[...], jnp.concatenate(sums, axis=0))
+    cell = lax.broadcasted_iota(jnp.int32, (owned, owned // POOL), 0)
+    voxel = lax.broadcasted_iota(jnp.int32, (owned, owned // POOL), 1)
+    pooled = exact_dot(mixed, (cell // POOL == voxel).astype(jnp.float32))
+    for b in range(rows // POOL):
+        out_ref[0, b] = pooled[b * DIRS : (b + 1) * DIRS]
+
+    for send in sends:
+        send.wait_send()
+    for p in range(slabs):
+        @pl.when(has_left)
+        def _():
+            to_left(p).wait_send()
+
+        @pl.when(has_right)
+        def _():
+            to_right(p).wait_send()
+
+
+def fused(slabs, tiles, volume):
+    planes, rows, cells = volume.shape
+    owned = cells // slabs
+    band = planes * RADIUS
+    body_rows = planes * rows
+    total = body_rows + 2 * band
+    wy = y_weights(owned)
+    wzx = zx_weights(planes, rows)
+    whist = histogram_weights(rows)
+    f32, bf16 = jnp.float32, jnp.bfloat16
+    dma = pltpu.SemaphoreType.DMA((slabs,))
+    halo = pltpu.VMEM((slabs, band + EDGE, owned), f32)
+    whole = pltpu.VMEM((slabs, body_rows + EDGE, owned), f32)
+    held = pltpu.VMEM(((slabs + 2) * total, 2 * owned), bf16)
+    return pl.pallas_call(
+        functools.partial(kernel, slabs, tiles),
+        out_shape=jax.ShapeDtypeStruct((1, rows // POOL, DIRS, owned // POOL), f32),
+        in_specs=[pl.BlockSpec(memory_space=pl.ANY)] * 3 + [pl.BlockSpec(memory_space=pltpu.VMEM)],
+        out_specs=pl.BlockSpec(memory_space=pltpu.VMEM),
+        scratch_shapes=[
+            pltpu.VMEM(volume.shape, f32),
+            pltpu.VMEM(wy.shape, bf16),
+            pltpu.VMEM(wzx.shape, bf16),
+            whole, whole, halo, halo, held, held,
+            pltpu.SemaphoreType.DMA((3,)),
+            dma, dma, dma, dma, dma, dma,
+        ],
+        compiler_params=pltpu.CompilerParams(
+            collective_id=0, has_side_effects=True, vmem_limit_bytes=40 * 1024 * 1024
+        ),
+    )(volume, jnp.asarray(wy), jnp.asarray(wzx), jnp.asarray(whist))
+
+
+def fits(slabs, tiles, planes, rows, cells):
+    owned = cells // slabs
+    return (
+        slabs * planes == POOL and planes >= RADIUS and planes * rows == LANES
+        and rows % POOL == 0 and rows >= 4 * RADIUS and (planes * RADIUS) % 16 == 0
+        and owned % LANES == 0 and slabs * EDGE <= LANES
+    )
+
+
 def solution(mesh):
+    slabs, tiles = mesh.shape["slab"], mesh.shape["tile"]
+
+    def whole(volume):
+        if slabs > 1 and tiles > 1 and fits(slabs, tiles, *volume.shape):
+            return fused(slabs, tiles, volume)
+        return body(volume)
+
     return jax.shard_map(
-        body,
+        whole,
         mesh=mesh,
         in_specs=(P("slab", "tile", None),),
         out_specs=P(None, "tile", None, "slab"),

time: 96 us -> 23.2 us (0.24)
  other arithmetic: 50.9 us -> 0 us
  Pallas kernels: 0 us -> 18 us
  waiting for transfers between devices: 17.2 us -> 0 us
  starting transfers between devices: 16 us -> 0 us
  local copies, waits for them, and re-layouts: 8.54 us -> 4.82 us
  between operations: 1.62 us -> 0.01 us
    add x5 -> x0, other arithmetic: 31.4 us -> none  [filtered(): total + weights[shift_index] * lax.slice_in_dim(padded, shift_index, shif...]
    pallas_call x0 -> x1, Pallas kernels: none -> 18 us  [fused(): pl.pallas_call(functools.partial(kernel, slabs, tiles), out_shape=jax.Sha...]
    reduce_sum x9 -> x0, other arithmetic: 16.6 us -> none  [the longest x7 15.3 us: pooled_full(): field.reshape(planes // POOL, POOL, rows // POOL, POOL, cells // POOL, POOL)]
    ppermute x4 -> x0, waiting for transfers between devices: 13.6 us -> none  [the longest x2 11.7 us: extended(): lax.ppermute(head, axis, [((i + 1) % count, i) for i in range(ends)])]
    ppermute x4 -> x0, starting transfers between devices: 11.8 us -> none  [the longest x2 8.57 us: extended(): lax.ppermute(tail, axis, [(i, (i + 1) % count) for i in range(ends)])]
    all_to_all x1 -> x0, starting transfers between devices: 4.27 us -> none  [body(): lax.all_to_all(volume, 'slab', split_axis=2, concat_axis=0, tiled=True)]
    all_to_all x1 -> x0, waiting for transfers between devices: 3.57 us -> none  [body(): lax.all_to_all(volume, 'slab', split_axis=2, concat_axis=0, tiled=True)]
    all_to_all x1 -> x0, other arithmetic: 2.14 us -> none  [body(): lax.all_to_all(volume, 'slab', split_axis=2, concat_axis=0, tiled=True)]
  transfers between devices with their start and end apart: 5 -> 0, of which waited for: 4 -> 0; matrix products, arithmetic and copies ran while one was open for 3% -> 0% of each run, Pallas kernels for 0% -> 0%
where the time goes in v1:
time: 23.2 us; the launch traced here: 22.9 us
  Pallas kernels  18 us (78%)
  local copies, waits for them, and re-layouts  4.82 us (21%)
    pallas_call x1, Pallas kernels, fused(): pl.pallas_call(functools.partial(kernel, slabs, tiles), out_shape=jax.Sha...  18 us
    unnamed x8, local copies, waits for them, and re-layouts  4.15 us
    pallas_call x1, local copies, waits for them, and re-layouts, fused(): pl.pallas_call(functools.partial(kernel, slabs, tiles), out_shape=jax.Sha...  0.68 us

profile of v1, /device:TPU:1, one launch (start us, length us, event | category | flops | bytes accessed | tf_op | source)
XLA Modules:
  0.0 22.9 jit_solution(2465763825725767336)
XLA Ops:
  0.0 0.0 copy-start
  0.0 1.1 %copy-done = bf16[2,384,480]{2,1,0:T(8,128)(2,1)S(1)} copy-done((bf16[2,384,480]{2,1,0:T(8,128)(2,1)S(1)}, bf16[2,384,480]{2,1,0:T(8,128)(2,1)}, u32[]{:S(2)}) %copy-start) | copy-done | bytes 737304
  1.1 0.0 copy-start.1
  1.1 1.1 %copy-done.1 = bf16[2,384,512]{2,1,0:T(8,128)(2,1)S(1)} copy-done((bf16[2,384,512]{2,1,0:T(8,128)(2,1)S(1)}, bf16[2,384,512]{2,1,0:T(8,128)(2,1)}, u32[]{:S(2)}) %copy-start.1) | copy-done | bytes 786456
  2.3 0.0 copy-start.2
  2.3 1.0 %copy-done.2 = f32[4,32,1024]{2,1,0:T(8,128)S(1)} copy-done((f32[4,32,1024]{2,1,0:T(8,128)S(1)}, f32[4,32,1024]{2,1,0:T(8,128)}, u32[]{:S(2)}) %copy-start.2) | copy-done | bytes 524312
  3.3 0.0 copy-start.3
  3.3 0.8 %copy-done.3 = f32[64,192]{1,0:T(8,128)S(1)} copy-done((f32[64,192]{1,0:T(8,128)S(1)}, f32[64,192]{1,0:T(8,128)}, u32[]{:S(2)}) %copy-start.3) | copy-done | bytes 49176
  4.2 18.0 %shard_map.46 = f32[1,2,32,16]{3,2,1,0:T(8,128)S(1)} custom-call(f32[4,32,1024]{2,1,0:T(8,128)S(1)} %copy-done.2, bf16[2,384,512]{2,1,0:T(8,128)(2,1)S(1)} %copy-done.1, bf16[2,384,480]{2,1,0:T(8,128)(2,1)S(1)} %copy-done, f32[64,192]{1,0:T(8,128)S(1)} %copy-done.3), custom_call_target="tpu_custom_call" | custom-call | tf_op jit(solution)/shard_map/pallas_call | solution.py:445
  22.2 0.7 %copy.5 = f32[1,2,32,16]{2,3,1,0:T(8,128)} copy(f32[1,2,32,16]{3,2,1,0:T(8,128)S(1)} %shard_map.46) | data formatting | bytes 8192 | tf_op jit(solution)/shard_map/pallas_call | solution.py:445
Async XLA Ops:
  0.0 1.1 %copy-start = (bf16[2,384,480]{2,1,0:T(8,128)(2,1)S(1)}, bf16[2,384,480]{2,1,0:T(8,128)(2,1)}, u32[]{:S(2)}) copy-start(bf16[2,384,480]{2,1,0:T(8,128)(2,1)} %constant.7.clone.wzx_hbm) | copy-start | bytes 2211844
  1.1 1.1 %copy-start.1 = (bf16[2,384,512]{2,1,0:T(8,128)(2,1)S(1)}, bf16[2,384,512]{2,1,0:T(8,128)(2,1)}, u32[]{:S(2)}) copy-start(bf16[2,384,512]{2,1,0:T(8,128)(2,1)} %constant.6.clone.wy_hbm) | copy-start | bytes 2359300
  2.3 1.0 %copy-start.2 = (f32[4,32,1024]{2,1,0:T(8,128)S(1)}, f32[4,32,1024]{2,1,0:T(8,128)}, u32[]{:S(2)}) copy-start(f32[4,32,1024]{2,1,0:T(8,128)} %x_hbm.1) | copy-start | bytes 1572868
  3.3 0.8 %copy-start.3 = (f32[64,192]{1,0:T(8,128)S(1)}, f32[64,192]{1,0:T(8,128)}, u32[]{:S(2)}) copy-start(f32[64,192]{1,0:T(8,128)} %constant.8.clone.whist_ref) | copy-start | bytes 147460

commit v2 on v1

--- a/solution.py
+++ b/solution.py
@@ -15,6 +15,7 @@
 MESH = pl.DeviceIdType.MESH
 LANES = 128
 EDGE = 2 * RADIUS
+END_PART = 4 * EDGE
 
 
 def extended(cells, sides, width):
@@ -157,14 +158,14 @@
     smooth, deriv = host_taps()
     edge = np.concatenate([np.arange(-RADIUS, 0), owned + np.arange(RADIUS)])
     out = np.arange(owned)
-    table = np.zeros((owned + LANES, 2 * owned))
-    for column, weights in enumerate((smooth, deriv)):
-        span = slice(column * owned, (column + 1) * owned)
-        table[:owned, span] = tap_at(weights, out[:, None] - out[None, :])
+    inner = halves(np.concatenate([tap_at(w, out[:, None] - out[None, :]) for w in (smooth, deriv)], axis=1))
+    outer = halves(np.concatenate([tap_at(w, edge[:, None] - out[None, :]) for w in (smooth, deriv)], axis=1))
+    ends = np.zeros((LANES, 2 * owned), ml_dtypes.bfloat16)
+    for part, which in enumerate((0, 0, 1)):
         for copy in range(3):
-            start = owned + copy * EDGE
-            table[start : start + EDGE, span] = tap_at(weights, edge[:, None] - out[None, :])
-    return halves(table)
+            start = part * END_PART + copy * EDGE
+            ends[start : start + EDGE] = outer[which]
+    return np.concatenate([inner[0], inner[1], ends], axis=0)
 
 
 def zx_weights(planes, rows):
@@ -203,8 +204,8 @@
 
 
 def kernel(
-    slabs, tiles, x_hbm, wy_hbm, wzx_hbm, whist_ref, out_ref,
-    x_ref, wy_ref, wzx_ref, stage, recv, halo_l, halo_r, y_high, y_low,
+    slabs, tiles, x_hbm, wy_hbm, wzx_hbm, whist_hbm, out_ref,
+    x_ref, wy_ref, wzx_ref, whist_ref, stage, recv, halo_l, halo_r, y_high, y_low,
     load_sem, send_sem, recv_sem, fl_send, fl_recv, fr_send, fr_recv,
 ):
     planes, rows, cells = x_ref.shape
@@ -221,7 +222,7 @@
 
     loads = [
         pltpu.make_async_copy(src, dst, load_sem.at[i])
-        for i, (src, dst) in enumerate(((x_hbm, x_ref), (wy_hbm, wy_ref), (wzx_hbm, wzx_ref)))
+        for i, (src, dst) in enumerate(((x_hbm, x_ref), (wy_hbm, wy_ref), (wzx_hbm, wzx_ref), (whist_hbm, whist_ref)))
     ]
     for load in loads:
         load.start()
@@ -365,8 +366,14 @@
         ).T
         ends = jnp.concatenate([ends, ends[e_at : e_at + band], ends[mid : mid + band]], axis=0)
         ends = jnp.where(own_edge, ends, 0.0)
-        high, low = split(jnp.concatenate([block, ends], axis=1))
-        result = dot(high, wy_ref[0]) + dot(low, wy_ref[0]) + dot(high, wy_ref[1])
+        high, low = split(ends)
+        high = high.astype(jnp.float32)
+        low = low.astype(jnp.float32)
+        ends = high + pltpu.roll(low, END_PART, 1) + pltpu.roll(high, 2 * END_PART, 1)
+        high, low = split(block)
+        inner, finer = wy_ref[0:owned], wy_ref[owned : 2 * owned]
+        result = dot(high, inner) + dot(low, inner) + dot(high, finer)
+        result = result + dot(ends.astype(jnp.bfloat16), wy_ref[2 * owned : 2 * owned + LANES])
         high, low = split(result)
         at = pl.ds(pl.multiple_of((p + 1) * total, 16), total)
         y_high[at, :] = high
@@ -409,6 +416,7 @@
         )
 
     sums = lax.fori_loop(0, slabs, group, tuple(sums))
+    loads[3].wait()
     mixed = exact_dot(whist_ref[...], jnp.concatenate(sums, axis=0))
     cell = lax.broadcasted_iota(jnp.int32, (owned, owned // POOL), 0)
     voxel = lax.broadcasted_iota(jnp.int32, (owned, owned // POOL), 1)
@@ -445,14 +453,15 @@
     return pl.pallas_call(
         functools.partial(kernel, slabs, tiles),
         out_shape=jax.ShapeDtypeStruct((1, rows // POOL, DIRS, owned // POOL), f32),
-        in_specs=[pl.BlockSpec(memory_space=pl.ANY)] * 3 + [pl.BlockSpec(memory_space=pltpu.VMEM)],
+        in_specs=[pl.BlockSpec(memory_space=pltpu.HBM)] * 4,
         out_specs=pl.BlockSpec(memory_space=pltpu.VMEM),
         scratch_shapes=[
             pltpu.VMEM(volume.shape, f32),
             pltpu.VMEM(wy.shape, bf16),
             pltpu.VMEM(wzx.shape, bf16),
+            pltpu.VMEM(whist.shape, f32),
             whole, whole, halo, halo, held, held,
-            pltpu.SemaphoreType.DMA((3,)),
+            pltpu.SemaphoreType.DMA((4,)),
             dma, dma, dma, dma, dma, dma,
         ],
         compiler_params=pltpu.CompilerParams(

time: 23.2 us -> 23.2 us (level)
  no operation moved by 1% of the time
where the time goes in v2:
time: 23.2 us; the launch traced here: 22.9 us
  Pallas kernels  18.1 us (78%)
  local copies, waits for them, and re-layouts  4.78 us (21%)
    pallas_call x1, Pallas kernels, fused(): pl.pallas_call(functools.partial(kernel, slabs, tiles), out_shape=jax.Sha...  18.1 us
    unnamed x8, local copies, waits for them, and re-layouts  4.1 us
    pallas_call x1, local copies, waits for them, and re-layouts, fused(): pl.pallas_call(functools.partial(kernel, slabs, tiles), out_shape=jax.Sha...  0.68 us

profile of v2, /device:TPU:1, one launch (start us, length us, event | category | flops | bytes accessed | tf_op | source)
XLA Modules:
  0.0 22.9 jit_solution(8021443810456140839)
XLA Ops:
  0.0 0.0 copy-start
  0.0 1.1 %copy-done = bf16[2,384,480]{2,1,0:T(8,128)(2,1)S(1)} copy-done((bf16[2,384,480]{2,1,0:T(8,128)(2,1)S(1)}, bf16[2,384,480]{2,1,0:T(8,128)(2,1)}, u32[]{:S(2)}) %copy-start) | copy-done | bytes 737304
  1.1 0.0 copy-start.1
  1.1 1.1 %copy-done.1 = bf16[640,512]{1,0:T(8,128)(2,1)S(1)} copy-done((bf16[640,512]{1,0:T(8,128)(2,1)S(1)}, bf16[640,512]{1,0:T(8,128)(2,1)}, u32[]{:S(2)}) %copy-start.1) | copy-done | bytes 655384
  2.2 0.0 copy-start.2
  2.2 1.0 %copy-done.2 = f32[4,32,1024]{2,1,0:T(8,128)S(1)} copy-done((f32[4,32,1024]{2,1,0:T(8,128)S(1)}, f32[4,32,1024]{2,1,0:T(8,128)}, u32[]{:S(2)}) %copy-start.2) | copy-done | bytes 524312
  3.3 0.0 copy-start.3
  3.3 0.8 %copy-done.3 = f32[64,192]{1,0:T(8,128)S(1)} copy-done((f32[64,192]{1,0:T(8,128)S(1)}, f32[64,192]{1,0:T(8,128)}, u32[]{:S(2)}) %copy-start.3) | copy-done | bytes 49176
  4.1 18.1 %shard_map.46 = f32[1,2,32,16]{3,2,1,0:T(8,128)S(1)} custom-call(f32[4,32,1024]{2,1,0:T(8,128)S(1)} %copy-done.2, bf16[640,512]{1,0:T(8,128)(2,1)S(1)} %copy-done.1, bf16[2,384,480]{2,1,0:T(8,128)(2,1)S(1)} %copy-done, f32[64,192]{1,0:T(8,128)S(1)} %copy-done.3), custom_call_target="tpu_custom_call" | custom-call | tf_op jit(solution)/shard_map/pallas_call | solution.py:453
  22.2 0.7 %copy.5 = f32[1,2,32,16]{2,3,1,0:T(8,128)} copy(f32[1,2,32,16]{3,2,1,0:T(8,128)S(1)} %shard_map.46) | data formatting | bytes 8192 | tf_op jit(solution)/shard_map/pallas_call | solution.py:453
Async XLA Ops:
  0.0 1.1 %copy-start = (bf16[2,384,480]{2,1,0:T(8,128)(2,1)S(1)}, bf16[2,384,480]{2,1,0:T(8,128)(2,1)}, u32[]{:S(2)}) copy-start(bf16[2,384,480]{2,1,0:T(8,128)(2,1)} %constant.7.clone.wzx_hbm) | copy-start | bytes 2211844
  1.1 1.1 %copy-start.1 = (bf16[640,512]{1,0:T(8,128)(2,1)S(1)}, bf16[640,512]{1,0:T(8,128)(2,1)}, u32[]{:S(2)}) copy-start(bf16[640,512]{1,0:T(8,128)(2,1)} %constant.6.clone.wy_hbm) | copy-start | bytes 1966084
  2.2 1.0 %copy-start.2 = (f32[4,32,1024]{2,1,0:T(8,128)S(1)}, f32[4,32,1024]{2,1,0:T(8,128)}, u32[]{:S(2)}) copy-start(f32[4,32,1024]{2,1,0:T(8,128)} %x_hbm.1) | copy-start | bytes 1572868
  3.3 0.8 %copy-start.3 = (f32[64,192]{1,0:T(8,128)S(1)}, f32[64,192]{1,0:T(8,128)}, u32[]{:S(2)}) copy-start(f32[64,192]{1,0:T(8,128)} %constant.8.clone.whist_hbm) | copy-start | bytes 147460

commit v3 on v2

v3 whole, which is shorter than its diff:
```python
import functools

import jax
import jax.numpy as jnp
import ml_dtypes
import numpy as np
from jax import lax
from jax.experimental import pallas as pl
from jax.experimental.pallas import tpu as pltpu
from jax.sharding import PartitionSpec as P

RADIUS = 4
POOL = 16
DIRS = 32
MESH = pl.DeviceIdType.MESH
LANES = 128
CHUNKS = 2
EDGE = 2 * RADIUS
END_PART = 4 * EDGE


def extended(cells, sides, width):
    for axis, dim in sides:
        count = lax.axis_size(axis)
        ends = count - 1
        head = lax.slice_in_dim(cells, 0, width, axis=dim)
        tail = lax.slice_in_dim(cells, cells.shape[dim] - width, cells.shape[dim], axis=dim)
        cells = jnp.concatenate(
            [
                lax.ppermute(tail, axis, [(i, (i + 1) % count) for i in range(ends)]),
                cells,
                lax.ppermute(head, axis, [((i + 1) % count, i) for i in range(ends)]),
            ],
            axis=dim,
        )
    return cells


def kernel_taps():
    offsets = jnp.arange(-RADIUS, RADIUS + 1).astype(jnp.float32)
    base = jnp.exp(-offsets * offsets / 8.0)
    smooth = base / jnp.sqrt(jnp.sum(base * base))
    slope = -offsets * base
    deriv = slope / jnp.sqrt(jnp.sum(slope * slope))
    return (smooth, deriv)


def direction_table():
    index = jnp.arange(DIRS).astype(jnp.float32)
    height = 1.0 - (index + 0.5) / DIRS
    radial = jnp.sqrt(1.0 - height * height)
    phase = 2.399963229728653 * index
    d_x = radial * jnp.cos(phase)
    d_y = radial * jnp.sin(phase)
    return jnp.stack(
        [
            height * height,
            2.0 * height * d_x,
            2.0 * height * d_y,
            d_x * d_x,
            2.0 * d_x * d_y,
            d_y * d_y,
        ],
        axis=1,
    )


def filtered(padded, weights, axis, count):
    total = weights[0] * lax.slice_in_dim(padded, 0, count, axis=axis)
    for shift_index in range(1, 2 * RADIUS + 1):
        total = total + weights[shift_index] * lax.slice_in_dim(
            padded, shift_index, shift_index + count, axis=axis
        )
    return total


def pooled_full(field):
    planes, rows, cells = field.shape
    return field.reshape(planes // POOL, POOL, rows // POOL, POOL, cells // POOL, POOL).sum(
        axis=(1, 3, 5)
    )


def body(volume):
    smooth, deriv = kernel_taps()
    planes, rows, cells = volume.shape
    coeffs = direction_table()
    regrouped = lax.all_to_all(volume, "slab", split_axis=2, concat_axis=0, tiled=True)
    depth = regrouped.shape[0]
    owned = regrouped.shape[2]
    padded = extended(regrouped, (("slab", 2), ("tile", 1)), RADIUS)
    zpad = jnp.pad(padded, ((RADIUS, RADIUS), (0, 0), (0, 0)))
    z_smooth = filtered(zpad, smooth, 0, depth)
    z_deriv = filtered(zpad, deriv, 0, depth)
    both_smooth = filtered(z_smooth, smooth, 1, rows)
    smooth_deriv = filtered(z_smooth, deriv, 1, rows)
    deriv_smooth = filtered(z_deriv, smooth, 1, rows)
    grad_y = filtered(both_smooth, deriv, 2, owned)
    grad_x = filtered(smooth_deriv, smooth, 2, owned)
    grad_z = filtered(deriv_smooth, smooth, 2, owned)
    tensor = jnp.stack(
        [
            pooled_full(grad_z * grad_z),
            pooled_full(grad_z * grad_x),
            pooled_full(grad_z * grad_y),
            pooled_full(grad_x * grad_x),
            pooled_full(grad_x * grad_y),
            pooled_full(grad_y * grad_y),
        ]
    )
    hist = jnp.einsum("kc,cabv->abkv", coeffs, tensor, precision=lax.Precision.HIGHEST)
    return hist / float(POOL**3)


def host_taps():
    offsets = np.arange(-RADIUS, RADIUS + 1).astype(np.float64)
    base = np.exp(-offsets * offsets / 8.0)
    slope = -offsets * base
    return base / np.sqrt(np.sum(base * base)), slope / np.sqrt(np.sum(slope * slope))


def host_directions():
    index = np.arange(DIRS).astype(np.float32)
    height = np.float32(1.0) - (index + np.float32(0.5)) / np.float32(DIRS)
    radial = np.sqrt(np.float32(1.0) - height * height)
    phase = np.float32(2.399963229728653) * index
    d_x = radial * np.cos(phase)
    d_y = radial * np.sin(phase)
    two = np.float32(2.0)
    return np.stack(
        [height * height, two * height * d_x, two * height * d_y, d_x * d_x, two * d_x * d_y, d_y * d_y],
        axis=1,
    ).astype(np.float32)


def tap_at(weights, distance):
    index = distance + RADIUS
    inside = (index >= 0) & (index <= 2 * RADIUS)
    return np.where(inside, weights[np.clip(index, 0, 2 * RADIUS)], 0.0)


def halves(matrix):
    high = matrix.astype(np.float32).astype(ml_dtypes.bfloat16)
    low = (matrix - high.astype(np.float64)).astype(np.float32).astype(ml_dtypes.bfloat16)
    return np.stack([high, low])


def y_weights(owned):
    smooth, deriv = host_taps()
    edge = np.concatenate([np.arange(-RADIUS, 0), owned + np.arange(RADIUS)])
    out = np.arange(owned)
    inner = halves(np.concatenate([tap_at(w, out[:, None] - out[None, :]) for w in (smooth, deriv)], axis=1))
    outer = halves(np.concatenate([tap_at(w, edge[:, None] - out[None, :]) for w in (smooth, deriv)], axis=1))
    ends = np.zeros((LANES, 2 * owned), ml_dtypes.bfloat16)
    for part, which in enumerate((0, 0, 1)):
        for copy in range(3):
            start = part * END_PART + copy * EDGE
            ends[start : start + EDGE] = outer[which]
    return np.concatenate([inner[0], inner[1], ends], axis=0)


def zx_weights(planes, rows):
    smooth, deriv = host_taps()
    z_out, x_out = (g.ravel()[:, None] for g in np.meshgrid(np.arange(planes), np.arange(rows), indexing="ij"))
    step = np.arange(EDGE)
    around = np.where(step < RADIUS, rows + step, step - EDGE)
    tables = []
    for places in (np.arange(rows), around):
        z_in, x_in = (g.ravel()[None, :] for g in np.meshgrid(np.arange(planes), places, indexing="ij"))
        fields = []
        for z_taps, x_taps in ((deriv, smooth), (smooth, deriv), (smooth, smooth)):
            blocks = [
                tap_at(z_taps, group * planes + z_in - z_out) * tap_at(x_taps, x_in - x_out)
                for group in (-1, 0, 1)
            ]
            fields.append(np.concatenate(blocks, axis=1))
        tables.append(halves(np.concatenate(fields, axis=0)))
    inner, outer = tables
    return inner, np.concatenate([outer[0], outer[0], outer[1]], axis=1)


def histogram_weights(rows):
    voxels = rows // POOL
    inside = (np.arange(rows)[None, :] // POOL == np.arange(voxels)[:, None]).astype(np.float32)
    table = host_directions()[None, :, :, None] * inside[:, None, None, :]
    return (table.reshape(voxels * DIRS, -1) / np.float32(POOL**3)).astype(np.float32)


def split(values):
    high = values.astype(jnp.bfloat16)
    low = (values - high.astype(jnp.float32)).astype(jnp.bfloat16)
    return high, low


def dot(a, b):
    return jnp.dot(a, b, preferred_element_type=jnp.float32)


def exact_dot(a, b):
    return jnp.dot(a, b, preferred_element_type=jnp.float32, precision=lax.Precision.HIGHEST)


def kernel(
    slabs, tiles, x_hbm, wy_hbm, wzx_hbm, wring_hbm, whist_hbm, out_ref,
    x_ref, wy_ref, wzx_ref, wring_ref, whist_ref,
    recv, halo_l, halo_r, ends_out, ends_in, ends_l, ends_r, ends_main, ends_ring,
    y_high, y_low, ring_high, ring_low, partial,
    load_sem, send_sem, recv_sem, end_send, end_recv, side_sem, fl_send, fl_recv, fr_send, fr_recv,
):
    planes, rows, cells = x_ref.shape
    owned = cells // slabs
    inner_rows = planes * rows
    ring_rows = planes * EDGE
    part = planes // CHUNKS
    s = lax.axis_index("slab")
    t = lax.axis_index("tile")
    has_left = t > 0
    has_right = t < tiles - 1

    pairs = (
        (x_hbm, x_ref), (wy_hbm, wy_ref), (wzx_hbm, wzx_ref), (wring_hbm, wring_ref), (whist_hbm, whist_ref)
    )
    loads = [pltpu.make_async_copy(src, dst, load_sem.at[i]) for i, (src, dst) in enumerate(pairs)]
    for load in loads:
        load.start()

    barrier = pltpu.get_barrier_semaphore()
    for k in range(1, slabs):
        pl.semaphore_signal(barrier, inc=1, device_id=(lax.rem(s + k, slabs), t), device_id_type=MESH)

    @pl.when(has_left)
    def _():
        pl.semaphore_signal(barrier, inc=1, device_id=(s, t - 1), device_id_type=MESH)

    @pl.when(has_right)
    def _():
        pl.semaphore_signal(barrier, inc=1, device_id=(s, t + 1), device_id_type=MESH)

    loads[0].wait()
    lane = lax.broadcasted_iota(jnp.int32, (inner_rows, LANES), 1)
    edges = jnp.zeros((inner_rows, LANES), jnp.float32)

    def side(d, first):
        if d < 0 or d >= slabs:
            return jnp.zeros((inner_rows, LANES), jnp.float32)
        return x_ref[:, :, first : first + LANES].reshape(inner_rows, LANES)

    for d in range(slabs):
        before = side(d - 1, d * owned - LANES)
        after = side(d + 1, (d + 1) * owned)
        both = jnp.where(lane >= LANES // 2, before, after)
        turned = pltpu.roll(both, d * EDGE + RADIUS, 1)
        edges = jnp.where(lane // EDGE == d, turned, edges)
    edges = edges.T
    for d in range(slabs):
        ends_out[d] = edges[d * EDGE : (d + 1) * EDGE]

    beside = jnp.where(has_left, 1, 0) + jnp.where(has_right, 1, 0)
    pl.semaphore_wait(barrier, slabs - 1 + beside)

    def ends_copy(src, dst, k):
        return pltpu.make_async_remote_copy(
            src_ref=ends_out.at[dst], dst_ref=ends_in.at[src],
            send_sem=end_send.at[k], recv_sem=end_recv.at[src],
            device_id=(dst, t), device_id_type=MESH,
        )

    def block_copy(src, dst, k, c):
        first = pl.multiple_of(dst * owned, LANES)
        return pltpu.make_async_remote_copy(
            src_ref=x_ref.at[pl.ds(c * part, part), :, pl.ds(first, owned)],
            dst_ref=recv.at[src, pl.ds(c * part, part)],
            send_sem=send_sem.at[k * CHUNKS + c], recv_sem=recv_sem.at[src * CHUNKS + c],
            device_id=(dst, t), device_id_type=MESH,
        )

    def ends_left():
        return pltpu.make_async_remote_copy(
            src_ref=ends_in, dst_ref=ends_r, send_sem=side_sem.at[0], recv_sem=side_sem.at[1],
            device_id=(s, t - 1), device_id_type=MESH,
        )

    def ends_right():
        return pltpu.make_async_remote_copy(
            src_ref=ends_in, dst_ref=ends_l, send_sem=side_sem.at[2], recv_sem=side_sem.at[3],
            device_id=(s, t + 1), device_id_type=MESH,
        )

    def to_left(p, c):
        here = pl.ds(c * part, part)
        return pltpu.make_async_remote_copy(
            src_ref=recv.at[p, here, pl.ds(0, EDGE)], dst_ref=halo_r.at[p, here],
            send_sem=fl_send.at[p * CHUNKS + c], recv_sem=fl_recv.at[p * CHUNKS + c],
            device_id=(s, t - 1), device_id_type=MESH,
        )

    def to_right(p, c):
        here = pl.ds(c * part, part)
        return pltpu.make_async_remote_copy(
            src_ref=recv.at[p, here, pl.ds(rows - EDGE, EDGE)], dst_ref=halo_l.at[p, here],
            send_sem=fr_send.at[p * CHUNKS + c], recv_sem=fr_recv.at[p * CHUNKS + c],
            device_id=(s, t + 1), device_id_type=MESH,
        )

    def forward(p, c):
        @pl.when(has_left)
        def _():
            to_left(p, c).start()

        @pl.when(has_right)
        def _():
            to_right(p, c).start()

    sends = [ends_copy(s, lax.rem(s + k, slabs), k) for k in range(1, slabs)]
    sends += [block_copy(s, lax.rem(s + k, slabs), k, c) for c in range(CHUNKS) for k in range(1, slabs)]
    for send in sends:
        send.start()

    recv[s] = x_ref[:, :, pl.ds(pl.multiple_of(s * owned, LANES), owned)]
    ends_in[s] = ends_out[s]
    for c in range(CHUNKS):
        forward(s, c)

    @pl.when(jnp.logical_not(has_left))
    def _():
        halo_l[...] = jnp.zeros_like(halo_l)
        ends_l[...] = jnp.zeros_like(ends_l)

    @pl.when(jnp.logical_not(has_right))
    def _():
        halo_r[...] = jnp.zeros_like(halo_r)
        ends_r[...] = jnp.zeros_like(ends_r)

    for ref, count in ((y_high, inner_rows), (y_low, inner_rows), (ring_high, ring_rows), (ring_low, ring_rows)):
        blank = jnp.zeros((count, 2 * owned), jnp.bfloat16)
        ref[0:count, :] = blank
        ref[(slabs + 1) * count : (slabs + 2) * count, :] = blank

    for k in range(1, slabs):
        p = lax.rem(s + slabs - k, slabs)
        ends_copy(p, p, 0).wait_recv()

    @pl.when(has_left)
    def _():
        ends_left().start()

    @pl.when(has_right)
    def _():
        ends_right().start()

    @pl.when(has_left)
    def _():
        ends_right().wait_recv()

    @pl.when(has_right)
    def _():
        ends_left().wait_recv()

    def packed(ends):
        high, low = split(ends)
        high = high.astype(jnp.float32)
        low = low.astype(jnp.float32)
        all_parts = high + pltpu.roll(low, END_PART, 1) + pltpu.roll(high, 2 * END_PART, 1)
        return all_parts.astype(jnp.bfloat16)

    ring_lane = lax.broadcasted_iota(jnp.int32, (planes, EDGE, LANES), 2) // EDGE
    ring_step = lax.broadcasted_iota(jnp.int32, (planes, EDGE, LANES), 1)
    rest = jnp.zeros((LANES - 3 * EDGE, LANES), jnp.float32)
    for p in range(slabs):
        turned = jnp.concatenate([ends_in[p], ends_l[p], ends_r[p], rest], axis=0).T
        ends_main[p] = packed(jnp.where(lane < EDGE, turned, 0.0))
        turned = turned.reshape(planes, rows, LANES)
        right = jnp.where(ring_lane == 2, turned[:, 0:EDGE], 0.0)
        left = jnp.where(ring_lane == 1, turned[:, rows - EDGE : rows], 0.0)
        ring = jnp.where(ring_step < RADIUS, right, left).reshape(ring_rows, LANES)
        ends_ring[p * ring_rows : (p + 1) * ring_rows, :] = packed(ring)

    loads[1].wait()

    def along_y(block, ends):
        high, low = split(block)
        inner, finer = wy_ref[0:owned], wy_ref[owned : 2 * owned]
        result = dot(high, inner) + dot(low, inner) + dot(high, finer)
        return split(result + dot(ends, wy_ref[2 * owned : 2 * owned + LANES]))

    def inner_along_y(p):
        high, low = along_y(recv[p].reshape(inner_rows, owned), ends_main[p])
        at = pl.ds(pl.multiple_of((p + 1) * inner_rows, 16), inner_rows)
        y_high[at, :] = high
        y_low[at, :] = low

    inner_along_y(s)
    for c in range(CHUNKS):
        for k in range(1, slabs):
            p = lax.rem(s + slabs - k, slabs)
            block_copy(p, p, 0, c).wait_recv()
            forward(p, c)
    for k in range(1, slabs):
        inner_along_y(lax.rem(s + slabs - k, slabs))

    smooth_y = slice(0, owned)
    deriv_y = slice(owned, 2 * owned)
    pair = slice(0, 2 * inner_rows)
    last = slice(2 * inner_rows, 3 * inner_rows)
    loads[2].wait()

    def inner_group(g, carry):
        at = pl.ds(pl.multiple_of(g * inner_rows, 16), 3 * inner_rows)
        for out, field in ((pair, smooth_y), (last, deriv_y)):
            high = y_high[at, field]
            low = y_low[at, field]
            coarse = wzx_ref[0, out, :]
            partial[g, out, :] = dot(coarse, high) + dot(coarse, low) + dot(wzx_ref[1, out, :], high)
        return carry

    lax.fori_loop(0, slabs, inner_group, 0)

    for p in range(slabs):
        for c in range(CHUNKS):
            @pl.when(has_left)
            def _():
                to_right(p, c).wait_recv()

            @pl.when(has_right)
            def _():
                to_left(p, c).wait_recv()

    step = lax.broadcasted_iota(jnp.int32, (slabs, planes, EDGE, owned), 2)
    ring = jnp.where(step < RADIUS, halo_r[...], halo_l[...]).reshape(slabs * ring_rows, owned)
    high, low = along_y(ring, ends_ring[...])
    ring_high[ring_rows : (slabs + 1) * ring_rows, :] = high
    ring_low[ring_rows : (slabs + 1) * ring_rows, :] = low
    loads[3].wait()

    def group(g, sums):
        at = pl.ds(pl.multiple_of(g * ring_rows, 16), 3 * ring_rows)

        def gradient(out, field):
            high = ring_high[at, field]
            low = ring_low[at, field]
            return partial[g, out, :] + dot(wring_ref[out, :], jnp.concatenate([high, low, high], axis=0))

        both = gradient(pair, smooth_y)
        grad_z = both[:inner_rows]
        grad_x = both[inner_rows:]
        grad_y = gradient(last, deriv_y)
        products = (
            grad_z * grad_z, grad_z * grad_x, grad_z * grad_y,
            grad_x * grad_x, grad_x * grad_y, grad_y * grad_y,
        )
        return tuple(
            held + product.reshape(planes, rows, owned).sum(axis=0)
            for held, product in zip(sums, products)
        )

    blank = jnp.zeros((rows, owned), jnp.float32)
    sums = lax.fori_loop(0, slabs, group, (blank,) * 6)
    loads[4].wait()
    mixed = exact_dot(whist_ref[...], jnp.concatenate(sums, axis=0))
    cell = lax.broadcasted_iota(jnp.int32, (owned, owned // POOL), 0)
    voxel = lax.broadcasted_iota(jnp.int32, (owned, owned // POOL), 1)
    pooled = exact_dot(mixed, (cell // POOL == voxel).astype(jnp.float32))
    for b in range(rows // POOL):
        out_ref[0, b] = pooled[b * DIRS : (b + 1) * DIRS]

    for send in sends:
        send.wait_send()

    @pl.when(has_left)
    def _():
        ends_left().wait_send()
        for p in range(slabs):
            for c in range(CHUNKS):
                to_left(p, c).wait_send()

    @pl.when(has_right)
    def _():
        ends_right().wait_send()
        for p in range(slabs):
            for c in range(CHUNKS):
                to_right(p, c).wait_send()


def fused(slabs, tiles, volume):
    planes, rows, cells = volume.shape
    owned = cells // slabs
    inner_rows = planes * rows
    ring_rows = planes * EDGE
    wy = y_weights(owned)
    wzx, wring = zx_weights(planes, rows)
    whist = histogram_weights(rows)
    f32, bf16 = jnp.float32, jnp.bfloat16
    one = pltpu.SemaphoreType.DMA((slabs,))
    many = pltpu.SemaphoreType.DMA((slabs * CHUNKS,))
    halo = pltpu.VMEM((slabs, planes, EDGE, owned), f32)
    ends = pltpu.VMEM((slabs, EDGE, LANES), f32)
    held = pltpu.VMEM(((slabs + 2) * inner_rows, 2 * owned), bf16)
    ring = pltpu.VMEM(((slabs + 2) * ring_rows, 2 * owned), bf16)
    return pl.pallas_call(
        functools.partial(kernel, slabs, tiles),
        out_shape=jax.ShapeDtypeStruct((1, rows // POOL, DIRS, owned // POOL), f32),
        in_specs=[pl.BlockSpec(memory_space=pl.ANY)] * 5,
        out_specs=pl.BlockSpec(memory_space=pltpu.VMEM),
        scratch_shapes=[
            pltpu.VMEM(volume.shape, f32),
            pltpu.VMEM(wy.shape, bf16),
            pltpu.VMEM(wzx.shape, bf16),
            pltpu.VMEM(wring.shape, bf16),
            pltpu.VMEM(whist.shape, f32),
            pltpu.VMEM((slabs, planes, rows, owned), f32),
            halo, halo, ends, ends, ends, ends,
            pltpu.VMEM((slabs, inner_rows, LANES), bf16),
            pltpu.VMEM((slabs * ring_rows, LANES), bf16),
            held, held, ring, ring,
            pltpu.VMEM((slabs, 3 * inner_rows, owned), f32),
            pltpu.SemaphoreType.DMA((5,)),
            many, many, one, one, pltpu.SemaphoreType.DMA((4,)), many, many, many, many,
        ],
        compiler_params=pltpu.CompilerParams(collective_id=0, has_side_effects=True),
    )(volume, jnp.asarray(wy), jnp.asarray(wzx), jnp.asarray(wring), jnp.asarray(whist))


def fits(slabs, tiles, planes, rows, cells):
    owned = cells // slabs
    return (
        slabs * planes == POOL and planes >= RADIUS and planes * rows == LANES
        and rows % POOL == 0 and planes % CHUNKS == 0 and (planes * EDGE) % 16 == 0
        and owned % LANES == 0 and slabs * EDGE <= LANES
    )


def solution(mesh):
    slabs, tiles = mesh.shape["slab"], mesh.shape["tile"]

    def whole(volume):
        if slabs > 1 and tiles > 1 and fits(slabs, tiles, *volume.shape):
            return fused(slabs, tiles, volume)
        return body(volume)

    return jax.shard_map(
        whole,
        mesh=mesh,
        in_specs=(P("slab", "tile", None),),
        out_specs=P(None, "tile", None, "slab"),
        check_vma=False,
    )
```

time: 23.2 us -> 19 us (0.82)
  local copies, waits for them, and re-layouts: 4.78 us -> 1.43 us
  Pallas kernels: 18.1 us -> 17.3 us
    unnamed x8 -> x0, local copies, waits for them, and re-layouts: 4.1 us -> none
    pallas_call x1, Pallas kernels: 18.1 us -> 17.3 us  [fused(): pl.pallas_call(functools.partial(kernel, slabs, tiles), out_shape=jax.Sha...]
    pallas_call x1, local copies, waits for them, and re-layouts: 0.68 us -> 1.43 us  [fused(): pl.pallas_call(functools.partial(kernel, slabs, tiles), out_shape=jax.Sha...]
where the time goes in v3:
time: 19 us; the launch traced here: 18.8 us
  Pallas kernels  17.3 us (91%)
  local copies, waits for them, and re-layouts  1.43 us (8%)
    pallas_call x1, Pallas kernels, fused(): pl.pallas_call(functools.partial(kernel, slabs, tiles), out_shape=jax.Sha...  17.3 us
    pallas_call x1, local copies, waits for them, and re-layouts, fused(): pl.pallas_call(functools.partial(kernel, slabs, tiles), out_shape=jax.Sha...  1.43 us

profile of v3, /device:TPU:1, one launch (start us, length us, event | category | flops | bytes accessed | tf_op | source)
XLA Modules:
  0.0 18.8 jit_solution(17206692952680522444)
XLA Ops:
  0.0 17.3 %shard_map.55 = f32[1,2,32,16]{3,2,1,0:T(8,128)} custom-call(f32[4,32,1024]{2,1,0:T(8,128)} %x_hbm.1, bf16[640,512]{1,0:T(8,128)(2,1)} %constant.8.clone.wy_hbm, bf16[2,384,384]{2,1,0:T(8,128)(2,1)} %constant.9.clone.wzx_hbm, bf16[384,288]{1,0:T(8,128)(2,1)} %constant.10.clone.wring_hbm, f32[64,192]{1,0:T(8,128)} %constant.11.clone.whist_hbm), custom_call_target="tpu_custom_call" | custom-call | tf_op jit(solution)/shard_map/pallas_call | solution.py:499
  17.3 1.4 %copy.6 = f32[1,2,32,16]{2,3,1,0:T(8,128)} copy(f32[1,2,32,16]{3,2,1,0:T(8,128)} %shard_map.55) | data formatting | bytes 8192 | tf_op jit(solution)/shard_map/pallas_call | solution.py:499

commit v4 on v3

--- a/solution.py
+++ b/solution.py
@@ -164,19 +164,16 @@
     z_out, x_out = (g.ravel()[:, None] for g in np.meshgrid(np.arange(planes), np.arange(rows), indexing="ij"))
     step = np.arange(EDGE)
     around = np.where(step < RADIUS, rows + step, step - EDGE)
-    tables = []
-    for places in (np.arange(rows), around):
-        z_in, x_in = (g.ravel()[None, :] for g in np.meshgrid(np.arange(planes), places, indexing="ij"))
-        fields = []
-        for z_taps, x_taps in ((deriv, smooth), (smooth, deriv), (smooth, smooth)):
-            blocks = [
-                tap_at(z_taps, group * planes + z_in - z_out) * tap_at(x_taps, x_in - x_out)
-                for group in (-1, 0, 1)
-            ]
-            fields.append(np.concatenate(blocks, axis=1))
-        tables.append(halves(np.concatenate(fields, axis=0)))
-    inner, outer = tables
-    return inner, np.concatenate([outer[0], outer[0], outer[1]], axis=1)
+    grids = [np.meshgrid(np.arange(planes), places, indexing="ij") for places in (np.arange(rows), around)]
+    z_in = np.concatenate([z.ravel() for z, _ in grids])[None, :]
+    x_in = np.concatenate([x.ravel() for _, x in grids])[None, :]
+    blocks = []
+    for fields in (((deriv, smooth), (smooth, deriv)), ((smooth, smooth),)):
+        for group in (-1, 0, 1):
+            for z_taps, x_taps in fields:
+                blocks.append(tap_at(z_taps, group * planes + z_in - z_out) * tap_at(x_taps, x_in - x_out))
+    high, low = halves(np.concatenate(blocks, axis=0))
+    return np.concatenate([high, high, low], axis=1)
 
 
 def histogram_weights(rows):
@@ -201,10 +198,9 @@
 
 
 def kernel(
-    slabs, tiles, x_hbm, wy_hbm, wzx_hbm, wring_hbm, whist_hbm, out_ref,
-    x_ref, wy_ref, wzx_ref, wring_ref, whist_ref,
-    recv, halo_l, halo_r, ends_out, ends_in, ends_l, ends_r, ends_main, ends_ring,
-    y_high, y_low, ring_high, ring_low, partial,
+    slabs, tiles, x_hbm, wy_hbm, wzx_hbm, whist_hbm, out_ref,
+    x_ref, wy_ref, wzx_ref, whist_ref,
+    recv, halo_l, halo_r, ends_out, ends_in, ends_l, ends_r, ends_all, partial,
     load_sem, send_sem, recv_sem, end_send, end_recv, side_sem, fl_send, fl_recv, fr_send, fr_recv,
 ):
     planes, rows, cells = x_ref.shape
@@ -218,7 +214,7 @@
     has_right = t < tiles - 1
 
     pairs = (
-        (x_hbm, x_ref), (wy_hbm, wy_ref), (wzx_hbm, wzx_ref), (wring_hbm, wring_ref), (whist_hbm, whist_ref)
+        (x_hbm, x_ref), (wy_hbm, wy_ref), (wzx_hbm, wzx_ref), (whist_hbm, whist_ref)
     )
     loads = [pltpu.make_async_copy(src, dst, load_sem.at[i]) for i, (src, dst) in enumerate(pairs)]
     for load in loads:
@@ -311,8 +307,16 @@
         def _():
             to_right(p, c).start()
 
-    sends = [ends_copy(s, lax.rem(s + k, slabs), k) for k in range(1, slabs)]
-    sends += [block_copy(s, lax.rem(s + k, slabs), k, c) for c in range(CHUNKS) for k in range(1, slabs)]
+    paired = slabs & (slabs - 1) == 0
+
+    def peer_to(k):
+        return s ^ k if paired else lax.rem(s + k, slabs)
+
+    def peer_from(k):
+        return s ^ k if paired else lax.rem(s + slabs - k, slabs)
+
+    sends = [ends_copy(s, peer_to(k), k) for k in range(1, slabs)]
+    sends += [block_copy(s, peer_to(k), k, c) for k in range(1, slabs) for c in range(CHUNKS)]
     for send in sends:
         send.start()
 
@@ -331,13 +335,9 @@
         halo_r[...] = jnp.zeros_like(halo_r)
         ends_r[...] = jnp.zeros_like(ends_r)
 
-    for ref, count in ((y_high, inner_rows), (y_low, inner_rows), (ring_high, ring_rows), (ring_low, ring_rows)):
-        blank = jnp.zeros((count, 2 * owned), jnp.bfloat16)
-        ref[0:count, :] = blank
-        ref[(slabs + 1) * count : (slabs + 2) * count, :] = blank
-
+    partial[...] = jnp.zeros_like(partial)
     for k in range(1, slabs):
-        p = lax.rem(s + slabs - k, slabs)
+        p = peer_from(k)
         ends_copy(p, p, 0).wait_recv()
 
     @pl.when(has_left)
@@ -368,54 +368,19 @@
     rest = jnp.zeros((LANES - 3 * EDGE, LANES), jnp.float32)
     for p in range(slabs):
         turned = jnp.concatenate([ends_in[p], ends_l[p], ends_r[p], rest], axis=0).T
-        ends_main[p] = packed(jnp.where(lane < EDGE, turned, 0.0))
+        ends_all[p, 0:inner_rows] = packed(jnp.where(lane < EDGE, turned, 0.0))
         turned = turned.reshape(planes, rows, LANES)
         right = jnp.where(ring_lane == 2, turned[:, 0:EDGE], 0.0)
         left = jnp.where(ring_lane == 1, turned[:, rows - EDGE : rows], 0.0)
         ring = jnp.where(ring_step < RADIUS, right, left).reshape(ring_rows, LANES)
-        ends_ring[p * ring_rows : (p + 1) * ring_rows, :] = packed(ring)
+        ends_all[p, inner_rows : inner_rows + ring_rows] = packed(ring)
 
     loads[1].wait()
-
-    def along_y(block, ends):
-        high, low = split(block)
-        inner, finer = wy_ref[0:owned], wy_ref[owned : 2 * owned]
-        result = dot(high, inner) + dot(low, inner) + dot(high, finer)
-        return split(result + dot(ends, wy_ref[2 * owned : 2 * owned + LANES]))
-
-    def inner_along_y(p):
-        high, low = along_y(recv[p].reshape(inner_rows, owned), ends_main[p])
-        at = pl.ds(pl.multiple_of((p + 1) * inner_rows, 16), inner_rows)
-        y_high[at, :] = high
-        y_low[at, :] = low
-
-    inner_along_y(s)
-    for c in range(CHUNKS):
-        for k in range(1, slabs):
-            p = lax.rem(s + slabs - k, slabs)
-            block_copy(p, p, 0, c).wait_recv()
-            forward(p, c)
-    for k in range(1, slabs):
-        inner_along_y(lax.rem(s + slabs - k, slabs))
-
-    smooth_y = slice(0, owned)
-    deriv_y = slice(owned, 2 * owned)
-    pair = slice(0, 2 * inner_rows)
-    last = slice(2 * inner_rows, 3 * inner_rows)
     loads[2].wait()
-
-    def inner_group(g, carry):
-        at = pl.ds(pl.multiple_of(g * inner_rows, 16), 3 * inner_rows)
-        for out, field in ((pair, smooth_y), (last, deriv_y)):
-            high = y_high[at, field]
-            low = y_low[at, field]
-            coarse = wzx_ref[0, out, :]
-            partial[g, out, :] = dot(coarse, high) + dot(coarse, low) + dot(wzx_ref[1, out, :], high)
-        return carry
-
-    lax.fori_loop(0, slabs, inner_group, 0)
-
-    for p in range(slabs):
+    step = lax.broadcasted_iota(jnp.int32, (planes, EDGE, owned), 1)
+    pair = 2 * inner_rows
+
+    def add_source(p):
         for c in range(CHUNKS):
             @pl.when(has_left)
             def _():
@@ -425,25 +390,36 @@
             def _():
                 to_left(p, c).wait_recv()
 
-    step = lax.broadcasted_iota(jnp.int32, (slabs, planes, EDGE, owned), 2)
-    ring = jnp.where(step < RADIUS, halo_r[...], halo_l[...]).reshape(slabs * ring_rows, owned)
-    high, low = along_y(ring, ends_ring[...])
-    ring_high[ring_rows : (slabs + 1) * ring_rows, :] = high
-    ring_low[ring_rows : (slabs + 1) * ring_rows, :] = low
-    loads[3].wait()
+        ring = jnp.where(step < RADIUS, halo_r[p], halo_l[p]).reshape(ring_rows, owned)
+        high, low = split(jnp.concatenate([recv[p].reshape(inner_rows, owned), ring], axis=0))
+        inner, finer = wy_ref[0:owned], wy_ref[owned : 2 * owned]
+        result = dot(high, inner) + dot(low, inner) + dot(high, finer)
+        result = result + dot(ends_all[p], wy_ref[2 * owned : 2 * owned + LANES])
+        high, low = split(result)
+        parts = jnp.concatenate([high, low, high], axis=0)
+        for out, count, first, field in ((0, pair, 0, 0), (pair, inner_rows, 3 * pair, owned)):
+            share = dot(wzx_ref[first : first + 3 * count, :], parts[:, field : field + owned])
+            for i in range(3):
+                partial[p + 2 - i, out : out + count, :] += share[i * count : (i + 1) * count]
+
+    def arrive(k):
+        p = peer_from(k)
+        for c in range(CHUNKS):
+            block_copy(p, p, 0, c).wait_recv()
+            forward(p, c)
+
+    add_source(s)
+    for k in range(1, slabs - 1):
+        arrive(k)
+    for k in range(1, slabs - 1):
+        add_source(peer_from(k))
+    arrive(slabs - 1)
+    add_source(peer_from(slabs - 1))
 
     def group(g, sums):
-        at = pl.ds(pl.multiple_of(g * ring_rows, 16), 3 * ring_rows)
-
-        def gradient(out, field):
-            high = ring_high[at, field]
-            low = ring_low[at, field]
-            return partial[g, out, :] + dot(wring_ref[out, :], jnp.concatenate([high, low, high], axis=0))
-
-        both = gradient(pair, smooth_y)
-        grad_z = both[:inner_rows]
-        grad_x = both[inner_rows:]
-        grad_y = gradient(last, deriv_y)
+        grad_z = partial[g + 1, 0:inner_rows, :]
+        grad_x = partial[g + 1, inner_rows:pair, :]
+        grad_y = partial[g + 1, pair : pair + inner_rows, :]
         products = (
             grad_z * grad_z, grad_z * grad_x, grad_z * grad_y,
             grad_x * grad_x, grad_x * grad_y, grad_y * grad_y,
@@ -455,13 +431,16 @@
 
     blank = jnp.zeros((rows, owned), jnp.float32)
     sums = lax.fori_loop(0, slabs, group, (blank,) * 6)
-    loads[4].wait()
+    loads[3].wait()
     mixed = exact_dot(whist_ref[...], jnp.concatenate(sums, axis=0))
-    cell = lax.broadcasted_iota(jnp.int32, (owned, owned // POOL), 0)
-    voxel = lax.broadcasted_iota(jnp.int32, (owned, owned // POOL), 1)
-    pooled = exact_dot(mixed, (cell // POOL == voxel).astype(jnp.float32))
+    voxel = lax.broadcasted_iota(jnp.int32, (owned // POOL, owned), 0)
+    cell = lax.broadcasted_iota(jnp.int32, (owned // POOL, owned), 1)
+    pooled = lax.dot_general(
+        (cell // POOL == voxel).astype(jnp.float32), mixed, (((1,), (1,)), ((), ())),
+        precision=lax.Precision.HIGHEST, preferred_element_type=jnp.float32,
+    )
     for b in range(rows // POOL):
-        out_ref[0, b] = pooled[b * DIRS : (b + 1) * DIRS]
+        out_ref[0, b] = pooled[:, b * DIRS : (b + 1) * DIRS]
 
     for send in sends:
         send.wait_send()
@@ -487,37 +466,33 @@
     inner_rows = planes * rows
     ring_rows = planes * EDGE
     wy = y_weights(owned)
-    wzx, wring = zx_weights(planes, rows)
+    wzx = zx_weights(planes, rows)
     whist = histogram_weights(rows)
     f32, bf16 = jnp.float32, jnp.bfloat16
     one = pltpu.SemaphoreType.DMA((slabs,))
     many = pltpu.SemaphoreType.DMA((slabs * CHUNKS,))
     halo = pltpu.VMEM((slabs, planes, EDGE, owned), f32)
     ends = pltpu.VMEM((slabs, EDGE, LANES), f32)
-    held = pltpu.VMEM(((slabs + 2) * inner_rows, 2 * owned), bf16)
-    ring = pltpu.VMEM(((slabs + 2) * ring_rows, 2 * owned), bf16)
-    return pl.pallas_call(
+    turned = pl.pallas_call(
         functools.partial(kernel, slabs, tiles),
-        out_shape=jax.ShapeDtypeStruct((1, rows // POOL, DIRS, owned // POOL), f32),
-        in_specs=[pl.BlockSpec(memory_space=pl.ANY)] * 5,
+        out_shape=jax.ShapeDtypeStruct((1, rows // POOL, owned // POOL, DIRS), f32),
+        in_specs=[pl.BlockSpec(memory_space=pl.ANY)] * 4,
         out_specs=pl.BlockSpec(memory_space=pltpu.VMEM),
         scratch_shapes=[
             pltpu.VMEM(volume.shape, f32),
             pltpu.VMEM(wy.shape, bf16),
             pltpu.VMEM(wzx.shape, bf16),
-            pltpu.VMEM(wring.shape, bf16),
             pltpu.VMEM(whist.shape, f32),
             pltpu.VMEM((slabs, planes, rows, owned), f32),
             halo, halo, ends, ends, ends, ends,
-            pltpu.VMEM((slabs, inner_rows, LANES), bf16),
-            pltpu.VMEM((slabs * ring_rows, LANES), bf16),
-            held, held, ring, ring,
-            pltpu.VMEM((slabs, 3 * inner_rows, owned), f32),
-            pltpu.SemaphoreType.DMA((5,)),
+            pltpu.VMEM((slabs, inner_rows + ring_rows, LANES), bf16),
+            pltpu.VMEM((slabs + 2, 3 * inner_rows, owned), f32),
+            pltpu.SemaphoreType.DMA((4,)),
             many, many, one, one, pltpu.SemaphoreType.DMA((4,)), many, many, many, many,
         ],
         compiler_params=pltpu.CompilerParams(collective_id=0, has_side_effects=True),
-    )(volume, jnp.asarray(wy), jnp.asarray(wzx), jnp.asarray(wring), jnp.asarray(whist))
+    )(volume, jnp.asarray(wy), jnp.asarray(wzx), jnp.asarray(whist))
+    return jnp.swapaxes(turned, 2, 3)
 
 
 def fits(slabs, tiles, planes, rows, cells):

time: 19 us -> 22.6 us (1.19)
  Pallas kernels: 17.3 us -> 21.1 us
    pallas_call x1, Pallas kernels: 17.3 us -> 21.1 us  [fused(): pl.pallas_call(functools.partial(kernel, slabs, tiles), out_shape=jax.Sha...]
    pallas_call x1 -> x0, local copies, waits for them, and re-layouts: 1.43 us -> none  [fused(): pl.pallas_call(functools.partial(kernel, slabs, tiles), out_shape=jax.Sha...]
    unnamed x0 -> x1, local copies, waits for them, and re-layouts: none -> 1.32 us
where the time goes in v4:
time: 22.6 us; the launch traced here: 22.4 us
  Pallas kernels  21.1 us (93%)
  local copies, waits for them, and re-layouts  1.32 us (6%)
    pallas_call x1, Pallas kernels, fused(): pl.pallas_call(functools.partial(kernel, slabs, tiles), out_shape=jax.Sha...  21.1 us
    unnamed x1, local copies, waits for them, and re-layouts  1.32 us

profile of v4, /device:TPU:1, one launch (start us, length us, event | category | flops | bytes accessed | tf_op | source)
XLA Modules:
  0.0 22.4 jit_solution(16412965816612669864)
XLA Ops:
  0.0 21.1 %shard_map.46 = f32[1,2,16,32]{3,2,1,0:T(8,128)} custom-call(f32[4,32,1024]{2,1,0:T(8,128)} %x_hbm.1, bf16[640,512]{1,0:T(8,128)(2,1)} %constant.6.clone.wy_hbm, bf16[1152,480]{1,0:T(8,128)(2,1)} %constant.7.clone.wzx_hbm, f32[64,192]{1,0:T(8,128)} %constant.8.clone.whist_hbm), custom_call_target="tpu_custom_call" | custom-call | tf_op jit(solution)/shard_map/pallas_call | solution.py:476
  21.1 1.3 %copy.6 = f32[1,2,32,16]{2,3,1,0:T(8,128)} copy(f32[1,2,32,16]{2,3,1,0:T(8,128)} %bitcast.1) | data formatting | bytes 8192

commit v5 on v3

--- a/solution.py
+++ b/solution.py
@@ -14,7 +14,8 @@
 DIRS = 32
 MESH = pl.DeviceIdType.MESH
 LANES = 128
-CHUNKS = 2
+CHUNKS = 1
+VMEM_LIMIT = 64 * 2**20 - 128 * 2**10
 EDGE = 2 * RADIUS
 END_PART = 4 * EDGE
 
@@ -218,7 +219,8 @@
     has_right = t < tiles - 1
 
     pairs = (
-        (x_hbm, x_ref), (wy_hbm, wy_ref), (wzx_hbm, wzx_ref), (wring_hbm, wring_ref), (whist_hbm, whist_ref)
+        (x_hbm, x_ref), (wy_hbm, wy_ref), (wzx_hbm, wzx_ref), (wring_hbm, wring_ref),
+        (whist_hbm.at[pl.ds(0, whist_ref.shape[0])], whist_ref),
     )
     loads = [pltpu.make_async_copy(src, dst, load_sem.at[i]) for i, (src, dst) in enumerate(pairs)]
     for load in loads:
@@ -311,8 +313,16 @@
         def _():
             to_right(p, c).start()
 
-    sends = [ends_copy(s, lax.rem(s + k, slabs), k) for k in range(1, slabs)]
-    sends += [block_copy(s, lax.rem(s + k, slabs), k, c) for c in range(CHUNKS) for k in range(1, slabs)]
+    paired = slabs & (slabs - 1) == 0
+
+    def peer_to(k):
+        return s ^ k if paired else lax.rem(s + k, slabs)
+
+    def peer_from(k):
+        return s ^ k if paired else lax.rem(s + slabs - k, slabs)
+
+    sends = [ends_copy(s, peer_to(k), k) for k in range(1, slabs)]
+    sends += [block_copy(s, peer_to(k), k, c) for k in range(1, slabs) for c in range(CHUNKS)]
     for send in sends:
         send.start()
 
@@ -337,7 +347,7 @@
         ref[(slabs + 1) * count : (slabs + 2) * count, :] = blank
 
     for k in range(1, slabs):
-        p = lax.rem(s + slabs - k, slabs)
+        p = peer_from(k)
         ends_copy(p, p, 0).wait_recv()
 
     @pl.when(has_left)
@@ -390,13 +400,15 @@
         y_low[at, :] = low
 
     inner_along_y(s)
-    for c in range(CHUNKS):
-        for k in range(1, slabs):
-            p = lax.rem(s + slabs - k, slabs)
+    for k in range(1, slabs):
+        p = peer_from(k)
+        for c in range(CHUNKS):
             block_copy(p, p, 0, c).wait_recv()
             forward(p, c)
-    for k in range(1, slabs):
-        inner_along_y(lax.rem(s + slabs - k, slabs))
+        if k == slabs - 2:
+            for earlier in range(1, slabs - 1):
+                inner_along_y(peer_from(earlier))
+    inner_along_y(peer_from(slabs - 1))
 
     smooth_y = slice(0, owned)
     deriv_y = slice(owned, 2 * owned)
@@ -489,6 +501,8 @@
     wy = y_weights(owned)
     wzx, wring = zx_weights(planes, rows)
     whist = histogram_weights(rows)
+    padded = np.zeros((1024, whist.shape[1]), np.float32)
+    padded[: whist.shape[0]] = whist
     f32, bf16 = jnp.float32, jnp.bfloat16
     one = pltpu.SemaphoreType.DMA((slabs,))
     many = pltpu.SemaphoreType.DMA((slabs * CHUNKS,))
@@ -516,8 +530,8 @@
             pltpu.SemaphoreType.DMA((5,)),
             many, many, one, one, pltpu.SemaphoreType.DMA((4,)), many, many, many, many,
         ],
-        compiler_params=pltpu.CompilerParams(collective_id=0, has_side_effects=True),
-    )(volume, jnp.asarray(wy), jnp.asarray(wzx), jnp.asarray(wring), jnp.asarray(whist))
+        compiler_params=pltpu.CompilerParams(collective_id=0, has_side_effects=True, vmem_limit_bytes=VMEM_LIMIT),
+    )(volume, jnp.asarray(wy), jnp.asarray(wzx), jnp.asarray(wring), jnp.asarray(padded))
 
 
 def fits(slabs, tiles, planes, rows, cells):

time: 19 us -> 19.6 us (1.032)
  Pallas kernels: 17.3 us -> 18 us
    pallas_call x1, Pallas kernels: 17.3 us -> 18 us  [fused(): pl.pallas_call(functools.partial(kernel, slabs, tiles), out_shape=jax.Sha...]
where the time goes in v5:
time: 19.6 us; the launch traced here: 19.4 us
  Pallas kernels  18 us (92%)
  local copies, waits for them, and re-layouts  1.43 us (7%)
    pallas_call x1, Pallas kernels, fused(): pl.pallas_call(functools.partial(kernel, slabs, tiles), out_shape=jax.Sha...  18 us
    pallas_call x1, local copies, waits for them, and re-layouts, fused(): pl.pallas_call(functools.partial(kernel, slabs, tiles), out_shape=jax.Sha...  1.43 us

profile of v5, /device:TPU:1, one launch (start us, length us, event | category | flops | bytes accessed | tf_op | source)
XLA Modules:
  0.0 19.4 jit_solution(17812611785781860994)
XLA Ops:
  0.0 18.0 %shard_map.55 = f32[1,2,32,16]{3,2,1,0:T(8,128)} custom-call(f32[4,32,1024]{2,1,0:T(8,128)} %x_hbm.1, bf16[640,512]{1,0:T(8,128)(2,1)} %constant.8.clone.wy_hbm, bf16[2,384,384]{2,1,0:T(8,128)(2,1)} %constant.9.clone.wzx_hbm, bf16[384,288]{1,0:T(8,128)(2,1)} %constant.10.clone.wring_hbm, f32[1024,192]{1,0:T(8,128)} %constant.11.clone.whist_hbm), custom_call_target="tpu_custom_call" | custom-call | tf_op jit(solution)/shard_map/pallas_call | solution.py:513
  18.0 1.4 %copy.6 = f32[1,2,32,16]{2,3,1,0:T(8,128)} copy(f32[1,2,32,16]{3,2,1,0:T(8,128)} %shard_map.55) | data formatting | bytes 8192 | tf_op jit(solution)/shard_map/pallas_call | solution.py:513

commit v6 on v5

--- a/solution.py
+++ b/solution.py
@@ -15,7 +15,6 @@
 MESH = pl.DeviceIdType.MESH
 LANES = 128
 CHUNKS = 1
-VMEM_LIMIT = 64 * 2**20 - 128 * 2**10
 EDGE = 2 * RADIUS
 END_PART = 4 * EDGE
 
@@ -177,6 +176,14 @@
             fields.append(np.concatenate(blocks, axis=1))
         tables.append(halves(np.concatenate(fields, axis=0)))
     inner, outer = tables
+    count = planes * rows
+    shares = [
+        inner[:, first:stop, i * count : (i + 1) * count]
+        for first, stop in ((0, 2 * count), (2 * count, 3 * count))
+        for i in range(3)
+    ]
+    shares = np.concatenate(shares, axis=1)
+    inner = np.concatenate([shares[0], shares[0], shares[1]], axis=1)
     return inner, np.concatenate([outer[0], outer[0], outer[1]], axis=1)
 
 
@@ -205,7 +212,7 @@
     slabs, tiles, x_hbm, wy_hbm, wzx_hbm, wring_hbm, whist_hbm, out_ref,
     x_ref, wy_ref, wzx_ref, wring_ref, whist_ref,
     recv, halo_l, halo_r, ends_out, ends_in, ends_l, ends_r, ends_main, ends_ring,
-    y_high, y_low, ring_high, ring_low, partial,
+    ring_high, ring_low, partial,
     load_sem, send_sem, recv_sem, end_send, end_recv, side_sem, fl_send, fl_recv, fr_send, fr_recv,
 ):
     planes, rows, cells = x_ref.shape
@@ -220,7 +227,7 @@
 
     pairs = (
         (x_hbm, x_ref), (wy_hbm, wy_ref), (wzx_hbm, wzx_ref), (wring_hbm, wring_ref),
-        (whist_hbm.at[pl.ds(0, whist_ref.shape[0])], whist_ref),
+        (whist_hbm, whist_ref),
     )
     loads = [pltpu.make_async_copy(src, dst, load_sem.at[i]) for i, (src, dst) in enumerate(pairs)]
     for load in loads:
@@ -323,7 +330,7 @@
 
     sends = [ends_copy(s, peer_to(k), k) for k in range(1, slabs)]
     sends += [block_copy(s, peer_to(k), k, c) for k in range(1, slabs) for c in range(CHUNKS)]
-    for send in sends:
+    for send in sends[: -CHUNKS]:
         send.start()
 
     recv[s] = x_ref[:, :, pl.ds(pl.multiple_of(s * owned, LANES), owned)]
@@ -341,7 +348,8 @@
         halo_r[...] = jnp.zeros_like(halo_r)
         ends_r[...] = jnp.zeros_like(ends_r)
 
-    for ref, count in ((y_high, inner_rows), (y_low, inner_rows), (ring_high, ring_rows), (ring_low, ring_rows)):
+    partial[...] = jnp.zeros_like(partial)
+    for ref, count in ((ring_high, ring_rows), (ring_low, ring_rows)):
         blank = jnp.zeros((count, 2 * owned), jnp.bfloat16)
         ref[0:count, :] = blank
         ref[(slabs + 1) * count : (slabs + 2) * count, :] = blank
@@ -385,7 +393,16 @@
         ring = jnp.where(ring_step < RADIUS, right, left).reshape(ring_rows, LANES)
         ends_ring[p * ring_rows : (p + 1) * ring_rows, :] = packed(ring)
 
+    for send in sends[: -CHUNKS]:
+        send.wait_send()
+    for send in sends[-CHUNKS:]:
+        send.start()
     loads[1].wait()
+    loads[2].wait()
+    smooth_y = slice(0, owned)
+    deriv_y = slice(owned, 2 * owned)
+    pair = slice(0, 2 * inner_rows)
+    last = slice(2 * inner_rows, 3 * inner_rows)
 
     def along_y(block, ends):
         high, low = split(block)
@@ -395,9 +412,12 @@
 
     def inner_along_y(p):
         high, low = along_y(recv[p].reshape(inner_rows, owned), ends_main[p])
-        at = pl.ds(pl.multiple_of((p + 1) * inner_rows, 16), inner_rows)
-        y_high[at, :] = high
-        y_low[at, :] = low
+        parts = jnp.concatenate([high, low, high], axis=0)
+        for out, first, field in ((pair, 0, smooth_y), (last, 6 * inner_rows, deriv_y)):
+            count = out.stop - out.start
+            share = dot(wzx_ref[first : first + 3 * count, :], parts[:, field])
+            for i in range(3):
+                partial[p + 2 - i, out, :] += share[i * count : (i + 1) * count]
 
     inner_along_y(s)
     for k in range(1, slabs):
@@ -410,23 +430,6 @@
                 inner_along_y(peer_from(earlier))
     inner_along_y(peer_from(slabs - 1))
 
-    smooth_y = slice(0, owned)
-    deriv_y = slice(owned, 2 * owned)
-    pair = slice(0, 2 * inner_rows)
-    last = slice(2 * inner_rows, 3 * inner_rows)
-    loads[2].wait()
-
-    def inner_group(g, carry):
-        at = pl.ds(pl.multiple_of(g * inner_rows, 16), 3 * inner_rows)
-        for out, field in ((pair, smooth_y), (last, deriv_y)):
-            high = y_high[at, field]
-            low = y_low[at, field]
-            coarse = wzx_ref[0, out, :]
-            partial[g, out, :] = dot(coarse, high) + dot(coarse, low) + dot(wzx_ref[1, out, :], high)
-        return carry
-
-    lax.fori_loop(0, slabs, inner_group, 0)
-
     for p in range(slabs):
         for c in range(CHUNKS):
             @pl.when(has_left)
@@ -450,7 +453,7 @@
         def gradient(out, field):
             high = ring_high[at, field]
             low = ring_low[at, field]
-            return partial[g, out, :] + dot(wring_ref[out, :], jnp.concatenate([high, low, high], axis=0))
+            return partial[g + 1, out, :] + dot(wring_ref[out, :], jnp.concatenate([high, low, high], axis=0))
 
         both = gradient(pair, smooth_y)
         grad_z = both[:inner_rows]
@@ -475,7 +478,7 @@
     for b in range(rows // POOL):
         out_ref[0, b] = pooled[b * DIRS : (b + 1) * DIRS]
 
-    for send in sends:
+    for send in sends[-CHUNKS:]:
         send.wait_send()
 
     @pl.when(has_left)
@@ -501,14 +504,11 @@
     wy = y_weights(owned)
     wzx, wring = zx_weights(planes, rows)
     whist = histogram_weights(rows)
-    padded = np.zeros((1024, whist.shape[1]), np.float32)
-    padded[: whist.shape[0]] = whist
     f32, bf16 = jnp.float32, jnp.bfloat16
     one = pltpu.SemaphoreType.DMA((slabs,))
     many = pltpu.SemaphoreType.DMA((slabs * CHUNKS,))
     halo = pltpu.VMEM((slabs, planes, EDGE, owned), f32)
     ends = pltpu.VMEM((slabs, EDGE, LANES), f32)
-    held = pltpu.VMEM(((slabs + 2) * inner_rows, 2 * owned), bf16)
     ring = pltpu.VMEM(((slabs + 2) * ring_rows, 2 * owned), bf16)
     return pl.pallas_call(
         functools.partial(kernel, slabs, tiles),
@@ -525,13 +525,13 @@
             halo, halo, ends, ends, ends, ends,
             pltpu.VMEM((slabs, inner_rows, LANES), bf16),
             pltpu.VMEM((slabs * ring_rows, LANES), bf16),
-            held, held, ring, ring,
-            pltpu.VMEM((slabs, 3 * inner_rows, owned), f32),
+            ring, ring,
+            pltpu.VMEM((slabs + 2, 3 * inner_rows, owned), f32),
             pltpu.SemaphoreType.DMA((5,)),
             many, many, one, one, pltpu.SemaphoreType.DMA((4,)), many, many, many, many,
         ],
-        compiler_params=pltpu.CompilerParams(collective_id=0, has_side_effects=True, vmem_limit_bytes=VMEM_LIMIT),
-    )(volume, jnp.asarray(wy), jnp.asarray(wzx), jnp.asarray(wring), jnp.asarray(padded))
+        compiler_params=pltpu.CompilerParams(collective_id=0, has_side_effects=True),
+    )(volume, jnp.asarray(wy), jnp.asarray(wzx), jnp.asarray(wring), jnp.asarray(whist))
 
 
 def fits(slabs, tiles, planes, rows, cells):

time: 19.6 us -> 19.5 us (level)
  the two profiles are of different devices: /device:TPU:1 before, /device:TPU:17 now
where the time goes in v6:
time: 19.5 us; the launch traced here: 19.3 us
  Pallas kernels  17.9 us (92%)
  local copies, waits for them, and re-layouts  1.43 us (7%)
    pallas_call x1, Pallas kernels, fused(): pl.pallas_call(functools.partial(kernel, slabs, tiles), out_shape=jax.Sha...  17.9 us
    pallas_call x1, local copies, waits for them, and re-layouts, fused(): pl.pallas_call(functools.partial(kernel, slabs, tiles), out_shape=jax.Sha...  1.43 us

profile of v6, /device:TPU:17, one launch (start us, length us, event | category | flops | bytes accessed | tf_op | source)
XLA Modules:
  0.0 19.3 jit_solution(13864421100556938233)
XLA Ops:
  0.0 17.9 %shard_map.55 = f32[1,2,32,16]{3,2,1,0:T(8,128)} custom-call(f32[4,32,1024]{2,1,0:T(8,128)} %x_hbm.1, bf16[640,512]{1,0:T(8,128)(2,1)} %constant.8.clone.wy_hbm, bf16[1152,384]{1,0:T(8,128)(2,1)} %constant.9.clone.wzx_hbm, bf16[384,288]{1,0:T(8,128)(2,1)} %constant.10.clone.wring_hbm, f32[64,192]{1,0:T(8,128)} %constant.11.clone.whist_hbm), custom_call_target="tpu_custom_call" | custom-call | tf_op jit(solution)/shard_map/pallas_call | solution.py:513
  17.9 1.4 %copy.6 = f32[1,2,32,16]{2,3,1,0:T(8,128)} copy(f32[1,2,32,16]{3,2,1,0:T(8,128)} %shard_map.55) | data formatting | bytes 8192 | tf_op jit(solution)/shard_map/pallas_call | solution.py:513

commit v7 on v3

--- a/solution.py
+++ b/solution.py
@@ -15,6 +15,8 @@
 MESH = pl.DeviceIdType.MESH
 LANES = 128
 CHUNKS = 2
+VMEM_LIMIT = 64 * 2**20 - 480 * 2**10
+TALL = 1024
 EDGE = 2 * RADIUS
 END_PART = 4 * EDGE
 
@@ -186,6 +188,12 @@
     return (table.reshape(voxels * DIRS, -1) / np.float32(POOL**3)).astype(np.float32)
 
 
+def tall(table):
+    rows = np.zeros((max(TALL, table.shape[0]), table.shape[1]), table.dtype)
+    rows[: table.shape[0]] = table
+    return rows
+
+
 def split(values):
     high = values.astype(jnp.bfloat16)
     low = (values - high.astype(jnp.float32)).astype(jnp.bfloat16)
@@ -218,7 +226,9 @@
     has_right = t < tiles - 1
 
     pairs = (
-        (x_hbm, x_ref), (wy_hbm, wy_ref), (wzx_hbm, wzx_ref), (wring_hbm, wring_ref), (whist_hbm, whist_ref)
+        (x_hbm, x_ref), (wy_hbm, wy_ref), (wzx_hbm, wzx_ref),
+        (wring_hbm.at[pl.ds(0, wring_ref.shape[0])], wring_ref),
+        (whist_hbm.at[pl.ds(0, whist_ref.shape[0])], whist_ref),
     )
     loads = [pltpu.make_async_copy(src, dst, load_sem.at[i]) for i, (src, dst) in enumerate(pairs)]
     for load in loads:
@@ -235,6 +245,66 @@
     @pl.when(has_right)
     def _():
         pl.semaphore_signal(barrier, inc=1, device_id=(s, t + 1), device_id_type=MESH)
+
+    beside = jnp.where(has_left, 1, 0) + jnp.where(has_right, 1, 0)
+    pl.semaphore_wait(barrier, slabs - 1 + beside)
+
+    def ends_copy(src, dst, k):
+        return pltpu.make_async_remote_copy(
+            src_ref=ends_out.at[dst], dst_ref=ends_in.at[src],
+            send_sem=end_send.at[k], recv_sem=end_recv.at[src],
+            device_id=(dst, t), device_id_type=MESH,
+        )
+
+    def block_copy(src, dst, k, c):
+        first = pl.multiple_of(dst * owned, LANES)
+        return pltpu.make_async_remote_copy(
+            src_ref=x_hbm.at[pl.ds(c * part, part), :, pl.ds(first, owned)],
+            dst_ref=recv.at[src, pl.ds(c * part, part)],
+            send_sem=send_sem.at[k * CHUNKS + c], recv_sem=recv_sem.at[src * CHUNKS + c],
+            device_id=(dst, t), device_id_type=MESH,
+        )
+
+    def ends_left():
+        return pltpu.make_async_remote_copy(
+            src_ref=ends_in, dst_ref=ends_r, send_sem=side_sem.at[0], recv_sem=side_sem.at[1],
+            device_id=(s, t - 1), device_id_type=MESH,
+        )
+
+    def ends_right():
+        return pltpu.make_async_remote_copy(
+            src_ref=ends_in, dst_ref=ends_l, send_sem=side_sem.at[2], recv_sem=side_sem.at[3],
+            device_id=(s, t + 1), device_id_type=MESH,
+        )
+
+    def to_left(p, c):
+        here = pl.ds(c * part, part)
+        return pltpu.make_async_remote_copy(
+            src_ref=recv.at[p, here, pl.ds(0, EDGE)], dst_ref=halo_r.at[p, here],
+            send_sem=fl_send.at[p * CHUNKS + c], recv_sem=fl_recv.at[p * CHUNKS + c],
+            device_id=(s, t - 1), device_id_type=MESH,
+        )
+
+    def to_right(p, c):
+        here = pl.ds(c * part, part)
+        return pltpu.make_async_remote_copy(
+            src_ref=recv.at[p, here, pl.ds(rows - EDGE, EDGE)], dst_ref=halo_l.at[p, here],
+            send_sem=fr_send.at[p * CHUNKS + c], recv_sem=fr_recv.at[p * CHUNKS + c],
+            device_id=(s, t + 1), device_id_type=MESH,
+        )
+
+    def forward(p, c):
+        @pl.when(has_left)
+        def _():
+            to_left(p, c).start()
+
+        @pl.when(has_right)
+        def _():
+            to_right(p, c).start()
+
+    sends = [block_copy(s, lax.rem(s + k, slabs), k, c) for c in range(CHUNKS) for k in range(1, slabs)]
+    for send in sends[: slabs - 1]:
+        send.start()
 
     loads[0].wait()
     lane = lax.broadcasted_iota(jnp.int32, (inner_rows, LANES), 1)
@@ -255,66 +325,10 @@
     for d in range(slabs):
         ends_out[d] = edges[d * EDGE : (d + 1) * EDGE]
 
-    beside = jnp.where(has_left, 1, 0) + jnp.where(has_right, 1, 0)
-    pl.semaphore_wait(barrier, slabs - 1 + beside)
-
-    def ends_copy(src, dst, k):
-        return pltpu.make_async_remote_copy(
-            src_ref=ends_out.at[dst], dst_ref=ends_in.at[src],
-            send_sem=end_send.at[k], recv_sem=end_recv.at[src],
-            device_id=(dst, t), device_id_type=MESH,
-        )
-
-    def block_copy(src, dst, k, c):
-        first = pl.multiple_of(dst * owned, LANES)
-        return pltpu.make_async_remote_copy(
-            src_ref=x_ref.at[pl.ds(c * part, part), :, pl.ds(first, owned)],
-            dst_ref=recv.at[src, pl.ds(c * part, part)],
-            send_sem=send_sem.at[k * CHUNKS + c], recv_sem=recv_sem.at[src * CHUNKS + c],
-            device_id=(dst, t), device_id_type=MESH,
-        )
-
-    def ends_left():
-        return pltpu.make_async_remote_copy(
-            src_ref=ends_in, dst_ref=ends_r, send_sem=side_sem.at[0], recv_sem=side_sem.at[1],
-            device_id=(s, t - 1), device_id_type=MESH,
-        )
-
-    def ends_right():
-        return pltpu.make_async_remote_copy(
-            src_ref=ends_in, dst_ref=ends_l, send_sem=side_sem.at[2], recv_sem=side_sem.at[3],
-            device_id=(s, t + 1), device_id_type=MESH,
-        )
-
-    def to_left(p, c):
-        here = pl.ds(c * part, part)
-        return pltpu.make_async_remote_copy(
-            src_ref=recv.at[p, here, pl.ds(0, EDGE)], dst_ref=halo_r.at[p, here],
-            send_sem=fl_send.at[p * CHUNKS + c], recv_sem=fl_recv.at[p * CHUNKS + c],
-            device_id=(s, t - 1), device_id_type=MESH,
-        )
-
-    def to_right(p, c):
-        here = pl.ds(c * part, part)
-        return pltpu.make_async_remote_copy(
-            src_ref=recv.at[p, here, pl.ds(rows - EDGE, EDGE)], dst_ref=halo_l.at[p, here],
-            send_sem=fr_send.at[p * CHUNKS + c], recv_sem=fr_recv.at[p * CHUNKS + c],
-            device_id=(s, t + 1), device_id_type=MESH,
-        )
-
-    def forward(p, c):
-        @pl.when(has_left)
-        def _():
-            to_left(p, c).start()
-
-        @pl.when(has_right)
-        def _():
-            to_right(p, c).start()
-
-    sends = [ends_copy(s, lax.rem(s + k, slabs), k) for k in range(1, slabs)]
-    sends += [block_copy(s, lax.rem(s + k, slabs), k, c) for c in range(CHUNKS) for k in range(1, slabs)]
-    for send in sends:
+    others = [ends_copy(s, lax.rem(s + k, slabs), k) for k in range(1, slabs)]
+    for send in others + sends[slabs - 1 :]:
         send.start()
+    sends += others
 
     recv[s] = x_ref[:, :, pl.ds(pl.multiple_of(s * owned, LANES), owned)]
     ends_in[s] = ends_out[s]
@@ -516,8 +530,8 @@
             pltpu.SemaphoreType.DMA((5,)),
             many, many, one, one, pltpu.SemaphoreType.DMA((4,)), many, many, many, many,
         ],
-        compiler_params=pltpu.CompilerParams(collective_id=0, has_side_effects=True),
-    )(volume, jnp.asarray(wy), jnp.asarray(wzx), jnp.asarray(wring), jnp.asarray(whist))
+        compiler_params=pltpu.CompilerParams(collective_id=0, has_side_effects=True, vmem_limit_bytes=VMEM_LIMIT),
+    )(volume, jnp.asarray(wy), jnp.asarray(wzx), jnp.asarray(tall(wring)), jnp.asarray(tall(whist)))
 
 
 def fits(slabs, tiles, planes, rows, cells):

time: 19 us -> 20 us (1.053)
  Pallas kernels: 17.3 us -> 18.4 us
    pallas_call x1, Pallas kernels: 17.3 us -> 18.4 us  [fused(): pl.pallas_call(functools.partial(kernel, slabs, tiles), out_shape=jax.Sha...]
where the time goes in v7:
time: 20 us; the launch traced here: 19.8 us
  Pallas kernels  18.4 us (92%)
  local copies, waits for them, and re-layouts  1.43 us (7%)
    pallas_call x1, Pallas kernels, fused(): pl.pallas_call(functools.partial(kernel, slabs, tiles), out_shape=jax.Sha...  18.4 us
    pallas_call x1, local copies, waits for them, and re-layouts, fused(): pl.pallas_call(functools.partial(kernel, slabs, tiles), out_shape=jax.Sha...  1.43 us

profile of v7, /device:TPU:1, one launch (start us, length us, event | category | flops | bytes accessed | tf_op | source)
XLA Modules:
  0.0 19.8 jit_solution(6119616083662304722)
XLA Ops:
  0.0 18.4 %shard_map.55 = f32[1,2,32,16]{3,2,1,0:T(8,128)} custom-call(f32[4,32,1024]{2,1,0:T(8,128)} %x_hbm.1, bf16[640,512]{1,0:T(8,128)(2,1)} %constant.8.clone.wy_hbm, bf16[2,384,384]{2,1,0:T(8,128)(2,1)} %constant.9.clone.wzx_hbm, bf16[1024,288]{1,0:T(8,128)(2,1)} %constant.10.clone.wring_hbm, f32[1024,192]{1,0:T(8,128)} %constant.11.clone.whist_hbm), custom_call_target="tpu_custom_call" | custom-call | tf_op jit(solution)/shard_map/pallas_call | solution.py:513
  18.4 1.4 %copy.6 = f32[1,2,32,16]{2,3,1,0:T(8,128)} copy(f32[1,2,32,16]{3,2,1,0:T(8,128)} %shard_map.55) | data formatting | bytes 8192 | tf_op jit(solution)/shard_map/pallas_call | solution.py:513

commit v8 on v3

--- a/solution.py
+++ b/solution.py
@@ -311,8 +311,16 @@
         def _():
             to_right(p, c).start()
 
-    sends = [ends_copy(s, lax.rem(s + k, slabs), k) for k in range(1, slabs)]
-    sends += [block_copy(s, lax.rem(s + k, slabs), k, c) for c in range(CHUNKS) for k in range(1, slabs)]
+    paired = slabs & (slabs - 1) == 0
+
+    def peer_to(k):
+        return s ^ k if paired else lax.rem(s + k, slabs)
+
+    def peer_from(k):
+        return s ^ k if paired else lax.rem(s + slabs - k, slabs)
+
+    sends = [ends_copy(s, peer_to(k), k) for k in range(1, slabs)]
+    sends += [block_copy(s, peer_to(k), k, c) for c in range(CHUNKS) for k in range(1, slabs)]
     for send in sends:
         send.start()
 
@@ -337,7 +345,7 @@
         ref[(slabs + 1) * count : (slabs + 2) * count, :] = blank
 
     for k in range(1, slabs):
-        p = lax.rem(s + slabs - k, slabs)
+        p = peer_from(k)
         ends_copy(p, p, 0).wait_recv()
 
     @pl.when(has_left)
@@ -392,11 +400,11 @@
     inner_along_y(s)
     for c in range(CHUNKS):
         for k in range(1, slabs):
-            p = lax.rem(s + slabs - k, slabs)
+            p = peer_from(k)
             block_copy(p, p, 0, c).wait_recv()
             forward(p, c)
     for k in range(1, slabs):
-        inner_along_y(lax.rem(s + slabs - k, slabs))
+        inner_along_y(peer_from(k))
 
     smooth_y = slice(0, owned)
     deriv_y = slice(owned, 2 * owned)

time: 19 us -> 19.7 us (1.037)
  Pallas kernels: 17.3 us -> 18.1 us
    pallas_call x1, Pallas kernels: 17.3 us -> 18.1 us  [fused(): pl.pallas_call(functools.partial(kernel, slabs, tiles), out_shape=jax.Sha...]
where the time goes in v8:
time: 19.7 us; the launch traced here: 19.5 us
  Pallas kernels  18.1 us (92%)
  local copies, waits for them, and re-layouts  1.43 us (7%)
    pallas_call x1, Pallas kernels, fused(): pl.pallas_call(functools.partial(kernel, slabs, tiles), out_shape=jax.Sha...  18.1 us
    pallas_call x1, local copies, waits for them, and re-layouts, fused(): pl.pallas_call(functools.partial(kernel, slabs, tiles), out_shape=jax.Sha...  1.43 us

profile of v8, /device:TPU:1, one launch (start us, length us, event | category | flops | bytes accessed | tf_op | source)
XLA Modules:
  0.0 19.5 jit_solution(2840891580212212196)
XLA Ops:
  0.0 18.1 %shard_map.55 = f32[1,2,32,16]{3,2,1,0:T(8,128)} custom-call(f32[4,32,1024]{2,1,0:T(8,128)} %x_hbm.1, bf16[640,512]{1,0:T(8,128)(2,1)} %constant.8.clone.wy_hbm, bf16[2,384,384]{2,1,0:T(8,128)(2,1)} %constant.9.clone.wzx_hbm, bf16[384,288]{1,0:T(8,128)(2,1)} %constant.10.clone.wring_hbm, f32[64,192]{1,0:T(8,128)} %constant.11.clone.whist_hbm), custom_call_target="tpu_custom_call" | custom-call | tf_op jit(solution)/shard_map/pallas_call | solution.py:507
  18.1 1.4 %copy.6 = f32[1,2,32,16]{2,3,1,0:T(8,128)} copy(f32[1,2,32,16]{3,2,1,0:T(8,128)} %shard_map.55) | data formatting | bytes 8192 | tf_op jit(solution)/shard_map/pallas_call | solution.py:507

commit v9 on v6

--- a/solution.py
+++ b/solution.py
@@ -14,7 +14,9 @@
 DIRS = 32
 MESH = pl.DeviceIdType.MESH
 LANES = 128
-CHUNKS = 1
+CHUNKS = 2
+VMEM_LIMIT = 64 * 2**20 - 940 * 2**10
+TALL = 1024
 EDGE = 2 * RADIUS
 END_PART = 4 * EDGE
 
@@ -194,6 +196,12 @@
     return (table.reshape(voxels * DIRS, -1) / np.float32(POOL**3)).astype(np.float32)
 
 
+def tall(table):
+    rows = np.zeros((max(TALL, table.shape[0]), table.shape[1]), table.dtype)
+    rows[: table.shape[0]] = table
+    return rows
+
+
 def split(values):
     high = values.astype(jnp.bfloat16)
     low = (values - high.astype(jnp.float32)).astype(jnp.bfloat16)
@@ -226,8 +234,8 @@
     has_right = t < tiles - 1
 
     pairs = (
-        (x_hbm, x_ref), (wy_hbm, wy_ref), (wzx_hbm, wzx_ref), (wring_hbm, wring_ref),
-        (whist_hbm, whist_ref),
+        (x_hbm, x_ref), (wy_hbm, wy_ref), (wzx_hbm, wzx_ref), (wring_hbm.at[pl.ds(0, wring_ref.shape[0])], wring_ref),
+        (whist_hbm.at[pl.ds(0, whist_ref.shape[0])], whist_ref),
     )
     loads = [pltpu.make_async_copy(src, dst, load_sem.at[i]) for i, (src, dst) in enumerate(pairs)]
     for load in loads:
@@ -329,8 +337,8 @@
         return s ^ k if paired else lax.rem(s + slabs - k, slabs)
 
     sends = [ends_copy(s, peer_to(k), k) for k in range(1, slabs)]
-    sends += [block_copy(s, peer_to(k), k, c) for k in range(1, slabs) for c in range(CHUNKS)]
-    for send in sends[: -CHUNKS]:
+    sends += [block_copy(s, peer_to(k), k, c) for c in range(CHUNKS) for k in range(1, slabs)]
+    for send in sends:
         send.start()
 
     recv[s] = x_ref[:, :, pl.ds(pl.multiple_of(s * owned, LANES), owned)]
@@ -393,10 +401,6 @@
         ring = jnp.where(ring_step < RADIUS, right, left).reshape(ring_rows, LANES)
         ends_ring[p * ring_rows : (p + 1) * ring_rows, :] = packed(ring)
 
-    for send in sends[: -CHUNKS]:
-        send.wait_send()
-    for send in sends[-CHUNKS:]:
-        send.start()
     loads[1].wait()
     loads[2].wait()
     smooth_y = slice(0, owned)
@@ -420,15 +424,13 @@
                 partial[p + 2 - i, out, :] += share[i * count : (i + 1) * count]
 
     inner_along_y(s)
-    for k in range(1, slabs):
-        p = peer_from(k)
-        for c in range(CHUNKS):
+    for c in range(CHUNKS):
+        for k in range(1, slabs):
+            p = peer_from(k)
             block_copy(p, p, 0, c).wait_recv()
             forward(p, c)
-        if k == slabs - 2:
-            for earlier in range(1, slabs - 1):
-                inner_along_y(peer_from(earlier))
-    inner_along_y(peer_from(slabs - 1))
+    for k in range(1, slabs):
+        inner_along_y(peer_from(k))
 
     for p in range(slabs):
         for c in range(CHUNKS):
@@ -478,7 +480,7 @@
     for b in range(rows // POOL):
         out_ref[0, b] = pooled[b * DIRS : (b + 1) * DIRS]
 
-    for send in sends[-CHUNKS:]:
+    for send in sends:
         send.wait_send()
 
     @pl.when(has_left)
@@ -530,8 +532,8 @@
             pltpu.SemaphoreType.DMA((5,)),
             many, many, one, one, pltpu.SemaphoreType.DMA((4,)), many, many, many, many,
         ],
-        compiler_params=pltpu.CompilerParams(collective_id=0, has_side_effects=True),
-    )(volume, jnp.asarray(wy), jnp.asarray(wzx), jnp.asarray(wring), jnp.asarray(whist))
+        compiler_params=pltpu.CompilerParams(collective_id=0, has_side_effects=True, vmem_limit_bytes=VMEM_LIMIT),
+    )(volume, jnp.asarray(wy), jnp.asarray(wzx), jnp.asarray(tall(wring)), jnp.asarray(tall(whist)))
 
 
 def fits(slabs, tiles, planes, rows, cells):

time: 19.5 us -> 19.7 us (1.010)
  the two profiles are of different devices: /device:TPU:17 before, /device:TPU:1 now
where the time goes in v9:
time: 19.7 us; the launch traced here: 19.5 us
  Pallas kernels  18.1 us (92%)
  local copies, waits for them, and re-layouts  1.43 us (7%)
    pallas_call x1, Pallas kernels, fused(): pl.pallas_call(functools.partial(kernel, slabs, tiles), out_shape=jax.Sha...  18.1 us
    pallas_call x1, local copies, waits for them, and re-layouts, fused(): pl.pallas_call(functools.partial(kernel, slabs, tiles), out_shape=jax.Sha...  1.43 us

profile of v9, /device:TPU:1, one launch (start us, length us, event | category | flops | bytes accessed | tf_op | source)
XLA Modules:
  0.0 19.5 jit_solution(11552844565767787005)
XLA Ops:
  0.0 18.1 %shard_map.55 = f32[1,2,32,16]{3,2,1,0:T(8,128)} custom-call(f32[4,32,1024]{2,1,0:T(8,128)} %x_hbm.1, bf16[640,512]{1,0:T(8,128)(2,1)} %constant.8.clone.wy_hbm, bf16[1152,384]{1,0:T(8,128)(2,1)} %constant.9.clone.wzx_hbm, bf16[1024,288]{1,0:T(8,128)(2,1)} %constant.10.clone.wring_hbm, f32[1024,192]{1,0:T(8,128)} %constant.11.clone.whist_hbm), custom_call_target="tpu_custom_call" | custom-call | tf_op jit(solution)/shard_map/pallas_call | solution.py:515
  18.1 1.4 %copy.6 = f32[1,2,32,16]{2,3,1,0:T(8,128)} copy(f32[1,2,32,16]{3,2,1,0:T(8,128)} %shard_map.55) | data formatting | bytes 8192 | tf_op jit(solution)/shard_map/pallas_call | solution.py:515

commit v10 on v3

--- a/solution.py
+++ b/solution.py
@@ -348,32 +348,16 @@
     def _():
         ends_right().start()
 
-    @pl.when(has_left)
-    def _():
-        ends_right().wait_recv()
-
-    @pl.when(has_right)
-    def _():
-        ends_left().wait_recv()
-
-    def packed(ends):
-        high, low = split(ends)
-        high = high.astype(jnp.float32)
-        low = low.astype(jnp.float32)
-        all_parts = high + pltpu.roll(low, END_PART, 1) + pltpu.roll(high, 2 * END_PART, 1)
-        return all_parts.astype(jnp.bfloat16)
-
-    ring_lane = lax.broadcasted_iota(jnp.int32, (planes, EDGE, LANES), 2) // EDGE
-    ring_step = lax.broadcasted_iota(jnp.int32, (planes, EDGE, LANES), 1)
-    rest = jnp.zeros((LANES - 3 * EDGE, LANES), jnp.float32)
+    def turned_parts(*kinds):
+        parts = [split(kind) for kind in kinds]
+        rest = [jnp.zeros((END_PART - len(kinds) * EDGE, LANES), jnp.float32)]
+        high = [part[0].astype(jnp.float32) for part in parts] + rest
+        low = [part[1].astype(jnp.float32) for part in parts] + rest
+        last = [jnp.zeros((LANES - 3 * END_PART, LANES), jnp.float32)]
+        return jnp.concatenate(high + low + high + last, axis=0).T
+
     for p in range(slabs):
-        turned = jnp.concatenate([ends_in[p], ends_l[p], ends_r[p], rest], axis=0).T
-        ends_main[p] = packed(jnp.where(lane < EDGE, turned, 0.0))
-        turned = turned.reshape(planes, rows, LANES)
-        right = jnp.where(ring_lane == 2, turned[:, 0:EDGE], 0.0)
-        left = jnp.where(ring_lane == 1, turned[:, rows - EDGE : rows], 0.0)
-        ring = jnp.where(ring_step < RADIUS, right, left).reshape(ring_rows, LANES)
-        ends_ring[p * ring_rows : (p + 1) * ring_rows, :] = packed(ring)
+        ends_main[p] = turned_parts(ends_in[p]).astype(jnp.bfloat16)
 
     loads[1].wait()
 
@@ -414,6 +398,23 @@
         return carry
 
     lax.fori_loop(0, slabs, inner_group, 0)
+
+    @pl.when(has_left)
+    def _():
+        ends_right().wait_recv()
+
+    @pl.when(has_right)
+    def _():
+        ends_left().wait_recv()
+
+    ring_place = lax.broadcasted_iota(jnp.int32, (planes, EDGE, LANES), 2) // EDGE % (END_PART // EDGE)
+    ring_step = lax.broadcasted_iota(jnp.int32, (planes, EDGE, LANES), 1)
+    for p in range(slabs):
+        turned = turned_parts(ends_l[p], ends_r[p]).reshape(planes, rows, LANES)
+        right = jnp.where(ring_place == 1, turned[:, 0:EDGE], 0.0)
+        left = jnp.where(ring_place == 0, turned[:, rows - EDGE : rows], 0.0)
+        ring = jnp.where(ring_step < RADIUS, right, left).reshape(ring_rows, LANES)
+        ends_ring[p * ring_rows : (p + 1) * ring_rows, :] = ring.astype(jnp.bfloat16)
 
     for p in range(slabs):
         for c in range(CHUNKS):

time: 19 us -> 19 us (level)
  no operation moved by 1% of the time
where the time goes in v10:
time: 19 us; the launch traced here: 18.8 us
  Pallas kernels  17.3 us (91%)
  local copies, waits for them, and re-layouts  1.43 us (8%)
    pallas_call x1, Pallas kernels, fused(): pl.pallas_call(functools.partial(kernel, slabs, tiles), out_shape=jax.Sha...  17.3 us
    pallas_call x1, local copies, waits for them, and re-layouts, fused(): pl.pallas_call(functools.partial(kernel, slabs, tiles), out_shape=jax.Sha...  1.43 us

profile of v10, /device:TPU:1, one launch (start us, length us, event | category | flops | bytes accessed | tf_op | source)
XLA Modules:
  0.0 18.8 jit_solution(4986535618039062)
XLA Ops:
  0.0 17.3 %shard_map.55 = f32[1,2,32,16]{3,2,1,0:T(8,128)} custom-call(f32[4,32,1024]{2,1,0:T(8,128)} %x_hbm.1, bf16[640,512]{1,0:T(8,128)(2,1)} %constant.8.clone.wy_hbm, bf16[2,384,384]{2,1,0:T(8,128)(2,1)} %constant.9.clone.wzx_hbm, bf16[384,288]{1,0:T(8,128)(2,1)} %constant.10.clone.wring_hbm, f32[64,192]{1,0:T(8,128)} %constant.11.clone.whist_hbm), custom_call_target="tpu_custom_call" | custom-call | tf_op jit(solution)/shard_map/pallas_call | solution.py:500
  17.3 1.4 %copy.6 = f32[1,2,32,16]{2,3,1,0:T(8,128)} copy(f32[1,2,32,16]{3,2,1,0:T(8,128)} %shard_map.55) | data formatting | bytes 8192 | tf_op jit(solution)/shard_map/pallas_call | solution.py:500

commit v11 on v10

--- a/solution.py
+++ b/solution.py
@@ -388,16 +388,16 @@
     last = slice(2 * inner_rows, 3 * inner_rows)
     loads[2].wait()
 
-    def inner_group(g, carry):
-        at = pl.ds(pl.multiple_of(g * inner_rows, 16), 3 * inner_rows)
+    def inner_group(g):
+        at = pl.ds(g * inner_rows, 3 * inner_rows)
         for out, field in ((pair, smooth_y), (last, deriv_y)):
             high = y_high[at, field]
             low = y_low[at, field]
             coarse = wzx_ref[0, out, :]
             partial[g, out, :] = dot(coarse, high) + dot(coarse, low) + dot(wzx_ref[1, out, :], high)
-        return carry
-
-    lax.fori_loop(0, slabs, inner_group, 0)
+
+    for g in range(slabs):
+        inner_group(g)
 
     @pl.when(has_left)
     def _():
@@ -434,7 +434,7 @@
     loads[3].wait()
 
     def group(g, sums):
-        at = pl.ds(pl.multiple_of(g * ring_rows, 16), 3 * ring_rows)
+        at = pl.ds(g * ring_rows, 3 * ring_rows)
 
         def gradient(out, field):
             high = ring_high[at, field]
@@ -455,7 +455,9 @@
         )
 
     blank = jnp.zeros((rows, owned), jnp.float32)
-    sums = lax.fori_loop(0, slabs, group, (blank,) * 6)
+    sums = (blank,) * 6
+    for g in range(slabs):
+        sums = group(g, sums)
     loads[4].wait()
     mixed = exact_dot(whist_ref[...], jnp.concatenate(sums, axis=0))
     cell = lax.broadcasted_iota(jnp.int32, (owned, owned // POOL), 0)

time: 19 us -> 18.4 us (0.968)
  Pallas kernels: 17.3 us -> 16.8 us
    pallas_call x1, Pallas kernels: 17.3 us -> 16.8 us  [fused(): pl.pallas_call(functools.partial(kernel, slabs, tiles), out_shape=jax.Sha...]
where the time goes in v11:
time: 18.4 us; the launch traced here: 18.2 us
  Pallas kernels  16.8 us (91%)
  local copies, waits for them, and re-layouts  1.43 us (8%)
    pallas_call x1, Pallas kernels, fused(): pl.pallas_call(functools.partial(kernel, slabs, tiles), out_shape=jax.Sha...  16.8 us
    pallas_call x1, local copies, waits for them, and re-layouts, fused(): pl.pallas_call(functools.partial(kernel, slabs, tiles), out_shape=jax.Sha...  1.43 us

profile of v11, /device:TPU:1, one launch (start us, length us, event | category | flops | bytes accessed | tf_op | source)
XLA Modules:
  0.0 18.2 jit_solution(11428560552479009891)
XLA Ops:
  0.0 16.8 %shard_map.55 = f32[1,2,32,16]{3,2,1,0:T(8,128)} custom-call(f32[4,32,1024]{2,1,0:T(8,128)} %x_hbm.1, bf16[640,512]{1,0:T(8,128)(2,1)} %constant.8.clone.wy_hbm, bf16[2,384,384]{2,1,0:T(8,128)(2,1)} %constant.9.clone.wzx_hbm, bf16[384,288]{1,0:T(8,128)(2,1)} %constant.10.clone.wring_hbm, f32[64,192]{1,0:T(8,128)} %constant.11.clone.whist_hbm), custom_call_target="tpu_custom_call" | custom-call | tf_op jit(solution)/shard_map/pallas_call | solution.py:502
  16.8 1.4 %copy.6 = f32[1,2,32,16]{2,3,1,0:T(8,128)} copy(f32[1,2,32,16]{3,2,1,0:T(8,128)} %shard_map.55) | data formatting | bytes 8192 | tf_op jit(solution)/shard_map/pallas_call | solution.py:502

commit v12 on v11

--- a/solution.py
+++ b/solution.py
@@ -196,8 +196,10 @@
     return jnp.dot(a, b, preferred_element_type=jnp.float32)
 
 
-def exact_dot(a, b):
-    return jnp.dot(a, b, preferred_element_type=jnp.float32, precision=lax.Precision.HIGHEST)
+def split_dot(a, b):
+    a_high, a_low = split(a)
+    b_high, b_low = split(b)
+    return dot(jnp.concatenate([a_high, a_high, a_low], axis=1), jnp.concatenate([b_high, b_low, b_high], axis=0))
 
 
 def kernel(
@@ -459,10 +461,10 @@
     for g in range(slabs):
         sums = group(g, sums)
     loads[4].wait()
-    mixed = exact_dot(whist_ref[...], jnp.concatenate(sums, axis=0))
+    mixed = split_dot(whist_ref[...], jnp.concatenate(sums, axis=0))
     cell = lax.broadcasted_iota(jnp.int32, (owned, owned // POOL), 0)
     voxel = lax.broadcasted_iota(jnp.int32, (owned, owned // POOL), 1)
-    pooled = exact_dot(mixed, (cell // POOL == voxel).astype(jnp.float32))
+    pooled = split_dot(mixed, (cell // POOL == voxel).astype(jnp.float32))
     for b in range(rows // POOL):
         out_ref[0, b] = pooled[b * DIRS : (b + 1) * DIRS]
 

time: 18.4 us -> 18.3 us (level)
  no operation moved by 1% of the time
where the time goes in v12:
time: 18.3 us; the launch traced here: 18.1 us
  Pallas kernels  16.7 us (91%)
  local copies, waits for them, and re-layouts  1.43 us (8%)
    pallas_call x1, Pallas kernels, fused(): pl.pallas_call(functools.partial(kernel, slabs, tiles), out_shape=jax.Sha...  16.7 us
    pallas_call x1, local copies, waits for them, and re-layouts, fused(): pl.pallas_call(functools.partial(kernel, slabs, tiles), out_shape=jax.Sha...  1.43 us

profile of v12, /device:TPU:1, one launch (start us, length us, event | category | flops | bytes accessed | tf_op | source)
XLA Modules:
  0.0 18.1 jit_solution(15497663422900962116)
XLA Ops:
  0.0 16.7 %shard_map.55 = f32[1,2,32,16]{3,2,1,0:T(8,128)} custom-call(f32[4,32,1024]{2,1,0:T(8,128)} %x_hbm.1, bf16[640,512]{1,0:T(8,128)(2,1)} %constant.8.clone.wy_hbm, bf16[2,384,384]{2,1,0:T(8,128)(2,1)} %constant.9.clone.wzx_hbm, bf16[384,288]{1,0:T(8,128)(2,1)} %constant.10.clone.wring_hbm, f32[64,192]{1,0:T(8,128)} %constant.11.clone.whist_hbm), custom_call_target="tpu_custom_call" | custom-call | tf_op jit(solution)/shard_map/pallas_call | solution.py:504
  16.7 1.4 %copy.6 = f32[1,2,32,16]{2,3,1,0:T(8,128)} copy(f32[1,2,32,16]{3,2,1,0:T(8,128)} %shard_map.55) | data formatting | bytes 8192 | tf_op jit(solution)/shard_map/pallas_call | solution.py:504
